TPU v7x, 512 devices: a whole 4x4x16 slice. The times are simulated.
512 devices in a mesh: row: 16 (over y, x), col: 16 (over z), depth: 2 (over core).
Axes of the slice: x: 4, y: 4, z: 16, core: 2. Of those that a mesh axis runs over, the one named last changes fastest.
Arguments:
- a_matrix: bfloat16 [8192, 8192], P('row', 'col'), may hold values from -6 to 6
- b_matrix: bfloat16 [8192, 8192], P('row', 'col'), may hold values from -0.0625 to 0.0625
- mask_a: int32 [64, 64], P('row', 'col'), may hold values from 0 to 1, as said below
- mask_b: int32 [64, 64], P('row', 'col'), may hold values from 0 to 1, as said below
Outputs:
- product: bfloat16 [8192, 8192], P('row', ('col', 'depth'))
- rms_norm: float32 [], replicated
Inputs may be any that keep to these rules, and one draw needn't show every extreme that they name: `mask_a`: 1 marks an occupied block; occupancy thins out with distance from the diagonal, and every diagonal block is occupied. `mask_b`: 1 marks an occupied block; occupancy thins out with distance from the diagonal, and every diagonal block is occupied.
All inputs are finite; a program needn't handle non-finite values.
Results may differ from a plain program's by a relative error of at most 0.001.
Values may be sent and summed in bfloat16 or wider, within the bound.
No kernel may reach another device: no remote copies, remote signals or barrier semaphores. Data moves between devices by JAX's collectives and lax.ppermute only.
A program may use at most 64 MiB of HBM per device.

v0:
```python
import jax
import jax.numpy as jnp
from jax import lax
from jax.sharding import PartitionSpec as P


def from_behind(value, axis, by):
    size = lax.axis_size(axis)
    return lax.ppermute(value, axis, [(i, (i + by) % size) for i in range(size)])


def apply_mask(panel, mask):
    blocks_r = mask.shape[0]
    blocks_c = mask.shape[1]
    size_r = panel.shape[0] // blocks_r
    size_c = panel.shape[1] // blocks_c
    shaped = (
        panel.reshape(blocks_r, size_r, blocks_c, size_c)
        * mask.astype(panel.dtype)[:, None, :, None]
    )
    return shaped.reshape(panel.shape)


def rotate_cols(pair, offset, count):
    for bit in range((count - 1).bit_length()):
        moved = from_behind((pair[0], pair[1]), "col", count - (1 << bit))
        take = offset >> bit & 1 == 1
        pair = (jnp.where(take, moved[0], pair[0]), jnp.where(take, moved[1], pair[1]))
    return pair


def rotate_rows(pair, offset, count):
    for bit in range((count - 1).bit_length()):
        moved = from_behind((pair[0], pair[1]), "row", count - (1 << bit))
        take = offset >> bit & 1 == 1
        pair = (jnp.where(take, moved[0], pair[0]), jnp.where(take, moved[1], pair[1]))
    return pair


def per_device(a_matrix, b_matrix, mask_a, mask_b):
    count = lax.axis_size("row")
    layers = lax.axis_size("depth")
    steps_layer = count // layers
    row_index = lax.axis_index("row")
    col_index = lax.axis_index("col")
    layer = lax.axis_index("depth")
    width = a_matrix.shape[0]
    total = jnp.zeros((width, b_matrix.shape[1]), jnp.float32)
    left = rotate_cols((a_matrix, mask_a), (row_index + layer * steps_layer) % count, count)
    right = rotate_rows((b_matrix, mask_b), (col_index + layer * steps_layer) % count, count)
    for step in range(steps_layer):
        total = total + jnp.dot(
            apply_mask(left[0], left[1]),
            apply_mask(right[0], right[1]),
            preferred_element_type=jnp.float32,
        )
        if step + 1 < steps_layer:
            left = from_behind((left[0], left[1]), "col", count - 1)
            right = from_behind((right[0], right[1]), "row", count - 1)
    share = b_matrix.shape[1] // layers
    squares = None
    whole_sum = lax.psum(total, "depth")
    part_sum = lax.dynamic_slice_in_dim(whole_sum, layer * share, share, 1)
    squares = lax.psum(jnp.sum(part_sum * part_sum), ("row", "col", "depth"))
    entries = float(width * count * (width * count))
    rms_norm = jnp.sqrt(squares / entries + 1e-06)
    return (part_sum.astype(jnp.bfloat16), rms_norm)


def solution(mesh):
    placed = (P("row", "col"), P("row", "col"), P("row", "col"), P("row", "col"))
    return jax.shard_map(
        per_device,
        mesh=mesh,
        in_specs=placed,
        out_specs=(P("row", ("col", "depth")), P()),
        check_vma=False,
    )
```

profile of v0, /device:TPU:1, one launch (start us, length us, event | category | flops | bytes accessed | tf_op | source)
XLA Modules:
  0.0 515.9 jit_solution(18209879784110913739)
XLA Ops:
  7.2 12.0 %collective-permute-start = (bf16[512,512]{1,0:T(8,128)(2,1)}, bf16[512,512]{1,0:T(8,128)(2,1)S(1)}, u32[]{:S(2)}, u32[]{:S(2)}) collective-permute-start(bf16[512,512]{1,0:T(8,128)(2,1)} %param.4), channel_id=1, source_target_pairs={{0,30},{2,0},{4,2},{6,4},{8,6},{10,8},{12,10},{14,12},{16,14},{18,... | collective-permute-start | bytes 1572872 | tf_op jit(solution)/shard_map/ppermute | solution.py:9
  19.2 6.8 %collective-permute-start.8 = (bf16[512,512]{1,0:T(8,128)(2,1)}, bf16[512,512]{1,0:T(8,128)(2,1)S(1)}, u32[]{:S(2)}, u32[]{:S(2)}) collective-permute-start(bf16[512,512]{1,0:T(8,128)(2,1)} %param.5), channel_id=1, source_target_pairs={{0,480},{32,0},{64,32},{96,64},{128,96},{160,128},{192,160},{224,1... | collective-permute-start | bytes 1572872 | tf_op jit(solution)/shard_map/ppermute | solution.py:9
  26.0 4.0 collective-permute-done
  31.2 4.4 collective-permute-start.1
  36.6 6.2 %collective-permute-start.9 = (bf16[512,512]{1,0:T(8,128)(2,1)S(1)}, bf16[512,512]{1,0:T(8,128)(2,1)S(1)}, u32[]{:S(2)}, u32[]{:S(2)}) collective-permute-start(bf16[512,512]{1,0:T(8,128)(2,1)S(1)} %broadcast_select_fusion), channel_id=1, source_target_pairs={{0,448},{32,480},{64,0},{96,32},{128,64},{160,96},{192,128},{224,1... | collective-permute-start | bytes 1572872 | tf_op jit(solution)/shard_map/ppermute | solution.py:9
  42.8 13.7 %collective-permute-done.1 = bf16[512,512]{1,0:T(8,128)(2,1)S(1)} collective-permute-done((bf16[512,512]{1,0:T(8,128)(2,1)S(1)}, bf16[512,512]{1,0:T(8,128)(2,1)S(1)}, u32[]{:S(2)}, u32[]{:S(2)}) %collective-permute-start.1) | collective-permute-done | bytes 524320 | tf_op jit(solution)/shard_map/ppermute | solution.py:9
  56.5 6.8 %collective-permute-start.2 = (bf16[512,512]{1,0:T(8,128)(2,1)S(1)}, bf16[512,512]{1,0:T(8,128)(2,1)S(1)}, u32[]{:S(2)}, u32[]{:S(2)}) collective-permute-start(bf16[512,512]{1,0:T(8,128)(2,1)S(1)} %broadcast_select_fusion.5), channel_id=1, source_target_pairs={{0,24},{2,26},{4,28},{6,30},{8,0},{10,2},{12,4},{14,6},{16,8},{18,... | collective-permute-start | bytes 1572872 | tf_op jit(solution)/shard_map/ppermute | solution.py:9
  63.5 4.6 collective-permute-start.10
  68.1 25.3 %collective-permute-done.2 = bf16[512,512]{1,0:T(8,128)(2,1)S(1)} collective-permute-done((bf16[512,512]{1,0:T(8,128)(2,1)S(1)}, bf16[512,512]{1,0:T(8,128)(2,1)S(1)}, u32[]{:S(2)}, u32[]{:S(2)}) %collective-permute-start.2) | collective-permute-done | bytes 524320 | tf_op jit(solution)/shard_map/ppermute | solution.py:9
  93.5 2.9 collective-permute-start.3
  96.5 4.8 collective-permute-start.11
  101.3 27.7 %collective-permute-done.3 = bf16[512,512]{1,0:T(8,128)(2,1)S(1)} collective-permute-done((bf16[512,512]{1,0:T(8,128)(2,1)S(1)}, bf16[512,512]{1,0:T(8,128)(2,1)S(1)}, u32[]{:S(2)}, u32[]{:S(2)}) %collective-permute-start.3) | collective-permute-done | bytes 524320 | tf_op jit(solution)/shard_map/ppermute | solution.py:9
  129.1 19.1 %collective-permute-start.16 = (bf16[512,512]{1,0:T(8,128)(2,1)S(1)}, bf16[512,512]{1,0:T(8,128)(2,1)S(1)}, u32[]{:S(2)}, u32[]{:S(2)}) collective-permute-start(bf16[512,512]{1,0:T(8,128)(2,1)S(1)} %broadcast_select_fusion.7), channel_id=1, source_target_pairs={{0,30},{2,0},{4,2},{6,4},{8,6},{10,8},{12,10},{14,12},{16,14},{18,... | collective-permute-start | bytes 1572872 | tf_op jit(solution)/shard_map/ppermute | solution.py:9
  148.3 5.8 %collective-permute-start.18 = (bf16[512,512]{1,0:T(8,128)(2,1)S(1)}, bf16[512,512]{1,0:T(8,128)(2,1)S(1)}, u32[]{:S(2)}, u32[]{:S(2)}) collective-permute-start(bf16[512,512]{1,0:T(8,128)(2,1)S(1)} %broadcast_select_fusion.3), channel_id=1, source_target_pairs={{0,480},{32,0},{64,32},{96,64},{128,96},{160,128},{192,160},{224,1... | collective-permute-start | bytes 1572872 | tf_op jit(solution)/shard_map/ppermute | solution.py:9
  154.1 3.5 collective-permute-start.12
  159.6 4.2 collective-permute-done.12
  163.8 5.4 %collective-permute-start.13 = (s32[4,4]{1,0:T(4,128)S(1)}, s32[4,4]{1,0:T(4,128)S(1)}, u32[]{:S(2)}, u32[]{:S(2)}) collective-permute-start(s32[4,4]{1,0:T(4,128)S(1)} %broadcast_select_fusion.8), channel_id=1, source_target_pairs={{0,448},{32,480},{64,0},{96,32},{128,64},{160,96},{192,128},{224,1... | collective-permute-start | bytes 200 | tf_op jit(solution)/shard_map/ppermute | solution.py:9
  169.2 7.9 %collective-permute-done.16 = bf16[512,512]{1,0:T(8,128)(2,1)S(1)} collective-permute-done((bf16[512,512]{1,0:T(8,128)(2,1)S(1)}, bf16[512,512]{1,0:T(8,128)(2,1)S(1)}, u32[]{:S(2)}, u32[]{:S(2)}) %collective-permute-start.16) | collective-permute-done | bytes 524320 | tf_op jit(solution)/shard_map/ppermute | solution.py:9
  177.1 11.5 %collective-permute-start.20 = (bf16[512,512]{1,0:T(8,128)(2,1)S(1)}, bf16[512,512]{1,0:T(8,128)(2,1)S(1)}, u32[]{:S(2)}, u32[]{:S(2)}) collective-permute-start(bf16[512,512]{1,0:T(8,128)(2,1)S(1)} %collective-permute-done.16), channel_id=1, source_target_pairs={{0,30},{2,0},{4,2},{6,4},{8,6},{10,8},{12,10},{14,12},{16,14},{18,... | collective-permute-start | bytes 1572872 | tf_op jit(solution)/shard_map/ppermute | solution.py:9
  188.6 4.1 collective-permute-start.22
  192.8 9.8 %collective-permute-start.5 = (s32[4,4]{1,0:T(4,128)S(1)}, s32[4,4]{1,0:T(4,128)S(1)}, u32[]{:S(2)}, u32[]{:S(2)}) collective-permute-start(s32[4,4]{1,0:T(4,128)S(1)} %broadcast_select_fusion.12), channel_id=1, source_target_pairs={{0,28},{2,30},{4,0},{6,2},{8,4},{10,6},{12,8},{14,10},{16,12},{18,... | collective-permute-start | bytes 200 | tf_op jit(solution)/shard_map/ppermute | solution.py:9
  204.5 5.9 %collective-permute-start.6 = (s32[4,4]{1,0:T(4,128)S(1)}, s32[4,4]{1,0:T(4,128)S(1)}, u32[]{:S(2)}, u32[]{:S(2)}) collective-permute-start(s32[4,4]{1,0:T(4,128)S(1)} %broadcast_select_fusion.13), channel_id=1, source_target_pairs={{0,24},{2,26},{4,28},{6,30},{8,0},{10,2},{12,4},{14,6},{16,8},{18,... | collective-permute-start | bytes 200 | tf_op jit(solution)/shard_map/ppermute | solution.py:9
  210.4 3.4 collective-permute-start.24
  213.9 4.5 collective-permute-start.26
  218.4 2.5 collective-permute-start.7
  222.9 8.5 %collective-permute-done.7 = s32[4,4]{1,0:T(4,128)S(1)} collective-permute-done((s32[4,4]{1,0:T(4,128)S(1)}, s32[4,4]{1,0:T(4,128)S(1)}, u32[]{:S(2)}, u32[]{:S(2)}) %collective-permute-start.7) | collective-permute-done | bytes 96 | tf_op jit(solution)/shard_map/ppermute | solution.py:9
  237.4 2.8 collective-permute-start.19
  242.5 3.9 collective-permute-done.19
  246.4 4.2 collective-permute-start.23
  250.6 3.1 collective-permute-start.25
  253.8 4.4 collective-permute-start.27
  258.3 3.1 collective-permute-start.29
  261.4 4.4 collective-permute-start.31
  265.9 3.1 collective-permute-start.33
  269.1 4.4 collective-permute-start.35
  273.6 3.1 collective-permute-start.37
  276.7 4.4 collective-permute-start.39
  281.2 3.1 collective-permute-start.41
  284.4 4.4 collective-permute-start.43
  290.4 3.1 collective-permute-start.32
  293.6 6.9 %collective-permute-start.34 = (bf16[512,512]{1,0:T(8,128)(2,1)S(1)}, bf16[512,512]{1,0:T(8,128)(2,1)S(1)}, u32[]{:S(2)}, u32[]{:S(2)}) collective-permute-start(bf16[512,512]{1,0:T(8,128)(2,1)S(1)} %collective-permute-done.30), channel_id=1, source_target_pairs={{0,480},{32,0},{64,32},{96,64},{128,96},{160,128},{192,160},{224,1... | collective-permute-start | bytes 1572872 | tf_op jit(solution)/shard_map/ppermute | solution.py:9
  306.7 7.1 %collective-permute-start.38 = (bf16[512,512]{1,0:T(8,128)(2,1)S(1)}, bf16[512,512]{1,0:T(8,128)(2,1)S(1)}, u32[]{:S(2)}, u32[]{:S(2)}) collective-permute-start(bf16[512,512]{1,0:T(8,128)(2,1)S(1)} %collective-permute-done.34), channel_id=1, source_target_pairs={{0,480},{32,0},{64,32},{96,64},{128,96},{160,128},{192,160},{224,1... | collective-permute-start | bytes 1572872 | tf_op jit(solution)/shard_map/ppermute | solution.py:9
  316.6 3.2 collective-permute-start.40
  319.8 4.5 collective-permute-done.38
  324.3 7.4 %collective-permute-start.42 = (bf16[512,512]{1,0:T(8,128)(2,1)S(1)}, bf16[512,512]{1,0:T(8,128)(2,1)S(1)}, u32[]{:S(2)}, u32[]{:S(2)}) collective-permute-start(bf16[512,512]{1,0:T(8,128)(2,1)S(1)} %collective-permute-done.38), channel_id=1, source_target_pairs={{0,480},{32,0},{64,32},{96,64},{128,96},{160,128},{192,160},{224,1... | collective-permute-start | bytes 1572872 | tf_op jit(solution)/shard_map/ppermute | solution.py:9
  333.5 7.8 %collective-permute-done.42 = bf16[512,512]{1,0:T(8,128)(2,1)S(1)} collective-permute-done((bf16[512,512]{1,0:T(8,128)(2,1)S(1)}, bf16[512,512]{1,0:T(8,128)(2,1)S(1)}, u32[]{:S(2)}, u32[]{:S(2)}) %collective-permute-start.42) | collective-permute-done | bytes 524320 | tf_op jit(solution)/shard_map/ppermute | solution.py:9
  343.1 55.7 %all-reduce.2.cloned.1.call-done = f32[512,512]{1,0:T(8,128)} async-done(((f32[512,512]{1,0:T(8,128)}), f32[512,512]{1,0:T(8,128)}) %all-reduce.2.cloned.1.call-update) | async-done | bytes 1048592 | tf_op jit(solution)/shard_map/psum | solution.py:62
  400.6 104.8 %psum.15 = f32[]{:T(128)} all-reduce(f32[]{:T(128)} %multiply_reduce_fusion), channel_id=1, replica_groups=mesh['row'=16,'col'=16,'depth'=2] {'row','col','depth'}, use_global_device_ids=true, to_apply=%region_2.3 | all-reduce | flops 1 | bytes 8 | tf_op jit(solution)/shard_map/psum | solution.py:64
  (106 shorter events, 34.1 us)
Async XLA Ops:
  7.2 391.7 %all-reduce.2.cloned.1.call-start = ((), (), s32[]{:S(2)}) async-start(), calls=%async_computation | async-start | bytes 2097152 | tf_op jit(solution)/shard_map/psum | solution.py:62
  7.2 22.8 %collective-permute-start = (bf16[512,512]{1,0:T(8,128)(2,1)}, bf16[512,512]{1,0:T(8,128)(2,1)S(1)}, u32[]{:S(2)}, u32[]{:S(2)}) collective-permute-start(bf16[512,512]{1,0:T(8,128)(2,1)} %param.4), channel_id=1, source_target_pairs={{0,30},{2,0},{4,2},{6,4},{8,6},{10,8},{12,10},{14,12},{16,14},{18,... | collective-permute-start | bytes 1572872 | tf_op jit(solution)/shard_map/ppermute | solution.py:9
  19.2 17.4 %collective-permute-start.8 = (bf16[512,512]{1,0:T(8,128)(2,1)}, bf16[512,512]{1,0:T(8,128)(2,1)S(1)}, u32[]{:S(2)}, u32[]{:S(2)}) collective-permute-start(bf16[512,512]{1,0:T(8,128)(2,1)} %param.5), channel_id=1, source_target_pairs={{0,480},{32,0},{64,32},{96,64},{128,96},{160,128},{192,160},{224,1... | collective-permute-start | bytes 1572872 | tf_op jit(solution)/shard_map/ppermute | solution.py:9
  26.0 10.5 %copy-start = (bf16[512,512]{1,0:T(8,128)(2,1)S(1)}, bf16[512,512]{1,0:T(8,128)(2,1)}, u32[]{:S(2)}) copy-start(bf16[512,512]{1,0:T(8,128)(2,1)} %param.5) | copy-start | bytes 1572868
  31.2 25.3 %collective-permute-start.1 = (bf16[512,512]{1,0:T(8,128)(2,1)S(1)}, bf16[512,512]{1,0:T(8,128)(2,1)S(1)}, u32[]{:S(2)}, u32[]{:S(2)}) collective-permute-start(bf16[512,512]{1,0:T(8,128)(2,1)S(1)} %broadcast_select_fusion.4), channel_id=1, source_target_pairs={{0,28},{2,30},{4,0},{6,2},{8,4},{10,6},{12,8},{14,10},{16,12},{18,... | collective-permute-start | bytes 1572872 | tf_op jit(solution)/shard_map/ppermute | solution.py:9
  36.6 26.7 %collective-permute-start.9 = (bf16[512,512]{1,0:T(8,128)(2,1)S(1)}, bf16[512,512]{1,0:T(8,128)(2,1)S(1)}, u32[]{:S(2)}, u32[]{:S(2)}) collective-permute-start(bf16[512,512]{1,0:T(8,128)(2,1)S(1)} %broadcast_select_fusion), channel_id=1, source_target_pairs={{0,448},{32,480},{64,0},{96,32},{128,64},{160,96},{192,128},{224,1... | collective-permute-start | bytes 1572872 | tf_op jit(solution)/shard_map/ppermute | solution.py:9
  56.5 36.9 %collective-permute-start.2 = (bf16[512,512]{1,0:T(8,128)(2,1)S(1)}, bf16[512,512]{1,0:T(8,128)(2,1)S(1)}, u32[]{:S(2)}, u32[]{:S(2)}) collective-permute-start(bf16[512,512]{1,0:T(8,128)(2,1)S(1)} %broadcast_select_fusion.5), channel_id=1, source_target_pairs={{0,24},{2,26},{4,28},{6,30},{8,0},{10,2},{12,4},{14,6},{16,8},{18,... | collective-permute-start | bytes 1572872 | tf_op jit(solution)/shard_map/ppermute | solution.py:9
  63.5 33.0 %collective-permute-start.10 = (bf16[512,512]{1,0:T(8,128)(2,1)S(1)}, bf16[512,512]{1,0:T(8,128)(2,1)S(1)}, u32[]{:S(2)}, u32[]{:S(2)}) collective-permute-start(bf16[512,512]{1,0:T(8,128)(2,1)S(1)} %broadcast_select_fusion.1), channel_id=1, source_target_pairs={{0,384},{32,416},{64,448},{96,480},{128,0},{160,32},{192,64},{224,... | collective-permute-start | bytes 1572872 | tf_op jit(solution)/shard_map/ppermute | solution.py:9
  93.5 35.6 %collective-permute-start.3 = (bf16[512,512]{1,0:T(8,128)(2,1)S(1)}, bf16[512,512]{1,0:T(8,128)(2,1)S(1)}, u32[]{:S(2)}, u32[]{:S(2)}) collective-permute-start(bf16[512,512]{1,0:T(8,128)(2,1)S(1)} %broadcast_select_fusion.6), channel_id=1, source_target_pairs={{0,16},{2,18},{4,20},{6,22},{8,24},{10,26},{12,28},{14,30},{16,0},... | collective-permute-start | bytes 1572872 | tf_op jit(solution)/shard_map/ppermute | solution.py:9
  96.5 51.7 %collective-permute-start.11 = (bf16[512,512]{1,0:T(8,128)(2,1)S(1)}, bf16[512,512]{1,0:T(8,128)(2,1)S(1)}, u32[]{:S(2)}, u32[]{:S(2)}) collective-permute-start(bf16[512,512]{1,0:T(8,128)(2,1)S(1)} %broadcast_select_fusion.2), channel_id=1, source_target_pairs={{0,256},{32,288},{64,320},{96,352},{128,384},{160,416},{192,448},{... | collective-permute-start | bytes 1572872 | tf_op jit(solution)/shard_map/ppermute | solution.py:9
  129.1 25.0 %copy-start.1 = (s32[4,4]{1,0:T(4,128)S(1)}, s32[4,4]{1,0:T(4,128)}, u32[]{:S(2)}) copy-start(s32[4,4]{1,0:T(4,128)} %param.7) | copy-start | bytes 196
  129.1 28.5 %copy-start.2 = (s32[4,4]{1,0:T(4,128)S(1)}, s32[4,4]{1,0:T(4,128)}, u32[]{:S(2)}) copy-start(s32[4,4]{1,0:T(4,128)} %param.6) | copy-start | bytes 196
  129.1 47.9 %collective-permute-start.16 = (bf16[512,512]{1,0:T(8,128)(2,1)S(1)}, bf16[512,512]{1,0:T(8,128)(2,1)S(1)}, u32[]{:S(2)}, u32[]{:S(2)}) collective-permute-start(bf16[512,512]{1,0:T(8,128)(2,1)S(1)} %broadcast_select_fusion.7), channel_id=1, source_target_pairs={{0,30},{2,0},{4,2},{6,4},{8,6},{10,8},{12,10},{14,12},{16,14},{18,... | collective-permute-start | bytes 1572872 | tf_op jit(solution)/shard_map/ppermute | solution.py:9
  148.3 40.3 %collective-permute-start.18 = (bf16[512,512]{1,0:T(8,128)(2,1)S(1)}, bf16[512,512]{1,0:T(8,128)(2,1)S(1)}, u32[]{:S(2)}, u32[]{:S(2)}) collective-permute-start(bf16[512,512]{1,0:T(8,128)(2,1)S(1)} %broadcast_select_fusion.3), channel_id=1, source_target_pairs={{0,480},{32,0},{64,32},{96,64},{128,96},{160,128},{192,160},{224,1... | collective-permute-start | bytes 1572872 | tf_op jit(solution)/shard_map/ppermute | solution.py:9
  154.1 9.6 %collective-permute-start.12 = (s32[4,4]{1,0:T(4,128)S(1)}, s32[4,4]{1,0:T(4,128)S(1)}, u32[]{:S(2)}, u32[]{:S(2)}) collective-permute-start(s32[4,4]{1,0:T(4,128)S(1)} %copy-done.1), channel_id=1, source_target_pairs={{0,480},{32,0},{64,32},{96,64},{128,96},{160,128},{192,160},{224,1... | collective-permute-start | bytes 200 | tf_op jit(solution)/shard_map/ppermute | solution.py:9
  157.6 35.2 %collective-permute-start.4 = (s32[4,4]{1,0:T(4,128)S(1)}, s32[4,4]{1,0:T(4,128)S(1)}, u32[]{:S(2)}, u32[]{:S(2)}) collective-permute-start(s32[4,4]{1,0:T(4,128)S(1)} %copy-done.2), channel_id=1, source_target_pairs={{0,30},{2,0},{4,2},{6,4},{8,6},{10,8},{12,10},{14,12},{16,14},{18,... | collective-permute-start | bytes 200 | tf_op jit(solution)/shard_map/ppermute | solution.py:9
  163.8 38.8 %collective-permute-start.13 = (s32[4,4]{1,0:T(4,128)S(1)}, s32[4,4]{1,0:T(4,128)S(1)}, u32[]{:S(2)}, u32[]{:S(2)}) collective-permute-start(s32[4,4]{1,0:T(4,128)S(1)} %broadcast_select_fusion.8), channel_id=1, source_target_pairs={{0,448},{32,480},{64,0},{96,32},{128,64},{160,96},{192,128},{224,1... | collective-permute-start | bytes 200 | tf_op jit(solution)/shard_map/ppermute | solution.py:9
  177.1 33.3 %collective-permute-start.20 = (bf16[512,512]{1,0:T(8,128)(2,1)S(1)}, bf16[512,512]{1,0:T(8,128)(2,1)S(1)}, u32[]{:S(2)}, u32[]{:S(2)}) collective-permute-start(bf16[512,512]{1,0:T(8,128)(2,1)S(1)} %collective-permute-done.16), channel_id=1, source_target_pairs={{0,30},{2,0},{4,2},{6,4},{8,6},{10,8},{12,10},{14,12},{16,14},{18,... | collective-permute-start | bytes 1572872 | tf_op jit(solution)/shard_map/ppermute | solution.py:9
  188.6 25.2 %collective-permute-start.22 = (bf16[512,512]{1,0:T(8,128)(2,1)S(1)}, bf16[512,512]{1,0:T(8,128)(2,1)S(1)}, u32[]{:S(2)}, u32[]{:S(2)}) collective-permute-start(bf16[512,512]{1,0:T(8,128)(2,1)S(1)} %collective-permute-done.18), channel_id=1, source_target_pairs={{0,480},{32,0},{64,32},{96,64},{128,96},{160,128},{192,160},{224,1... | collective-permute-start | bytes 1572872 | tf_op jit(solution)/shard_map/ppermute | solution.py:9
  192.8 11.7 %collective-permute-start.5 = (s32[4,4]{1,0:T(4,128)S(1)}, s32[4,4]{1,0:T(4,128)S(1)}, u32[]{:S(2)}, u32[]{:S(2)}) collective-permute-start(s32[4,4]{1,0:T(4,128)S(1)} %broadcast_select_fusion.12), channel_id=1, source_target_pairs={{0,28},{2,30},{4,0},{6,2},{8,4},{10,6},{12,8},{14,10},{16,12},{18,... | collective-permute-start | bytes 200 | tf_op jit(solution)/shard_map/ppermute | solution.py:9
  202.6 18.4 %collective-permute-start.14 = (s32[4,4]{1,0:T(4,128)S(1)}, s32[4,4]{1,0:T(4,128)S(1)}, u32[]{:S(2)}, u32[]{:S(2)}) collective-permute-start(s32[4,4]{1,0:T(4,128)S(1)} %broadcast_select_fusion.9), channel_id=1, source_target_pairs={{0,384},{32,416},{64,448},{96,480},{128,0},{160,32},{192,64},{224,... | collective-permute-start | bytes 200 | tf_op jit(solution)/shard_map/ppermute | solution.py:9
  204.5 13.8 %collective-permute-start.6 = (s32[4,4]{1,0:T(4,128)S(1)}, s32[4,4]{1,0:T(4,128)S(1)}, u32[]{:S(2)}, u32[]{:S(2)}) collective-permute-start(s32[4,4]{1,0:T(4,128)S(1)} %broadcast_select_fusion.13), channel_id=1, source_target_pairs={{0,24},{2,26},{4,28},{6,30},{8,0},{10,2},{12,4},{14,6},{16,8},{18,... | collective-permute-start | bytes 200 | tf_op jit(solution)/shard_map/ppermute | solution.py:9
  210.4 22.9 %collective-permute-start.24 = (bf16[512,512]{1,0:T(8,128)(2,1)S(1)}, bf16[512,512]{1,0:T(8,128)(2,1)S(1)}, u32[]{:S(2)}, u32[]{:S(2)}) collective-permute-start(bf16[512,512]{1,0:T(8,128)(2,1)S(1)} %collective-permute-done.20), channel_id=1, source_target_pairs={{0,30},{2,0},{4,2},{6,4},{8,6},{10,8},{12,10},{14,12},{16,14},{18,... | collective-permute-start | bytes 1572872 | tf_op jit(solution)/shard_map/ppermute | solution.py:9
  213.9 21.5 %collective-permute-start.26 = (bf16[512,512]{1,0:T(8,128)(2,1)S(1)}, bf16[512,512]{1,0:T(8,128)(2,1)S(1)}, u32[]{:S(2)}, u32[]{:S(2)}) collective-permute-start(bf16[512,512]{1,0:T(8,128)(2,1)S(1)} %collective-permute-done.22), channel_id=1, source_target_pairs={{0,480},{32,0},{64,32},{96,64},{128,96},{160,128},{192,160},{224,1... | collective-permute-start | bytes 1572872 | tf_op jit(solution)/shard_map/ppermute | solution.py:9
  218.4 13.0 %collective-permute-start.7 = (s32[4,4]{1,0:T(4,128)S(1)}, s32[4,4]{1,0:T(4,128)S(1)}, u32[]{:S(2)}, u32[]{:S(2)}) collective-permute-start(s32[4,4]{1,0:T(4,128)S(1)} %broadcast_select_fusion.14), channel_id=1, source_target_pairs={{0,16},{2,18},{4,20},{6,22},{8,24},{10,26},{12,28},{14,30},{16,0},... | collective-permute-start | bytes 200 | tf_op jit(solution)/shard_map/ppermute | solution.py:9
  221.0 16.4 %collective-permute-start.15 = (s32[4,4]{1,0:T(4,128)S(1)}, s32[4,4]{1,0:T(4,128)S(1)}, u32[]{:S(2)}, u32[]{:S(2)}) collective-permute-start(s32[4,4]{1,0:T(4,128)S(1)} %broadcast_select_fusion.10), channel_id=1, source_target_pairs={{0,256},{32,288},{64,320},{96,352},{128,384},{160,416},{192,448},{... | collective-permute-start | bytes 200 | tf_op jit(solution)/shard_map/ppermute | solution.py:9
  231.4 8.8 %collective-permute-start.17 = (s32[4,4]{1,0:T(4,128)S(1)}, s32[4,4]{1,0:T(4,128)S(1)}, u32[]{:S(2)}, u32[]{:S(2)}) collective-permute-start(s32[4,4]{1,0:T(4,128)S(1)} %get-tuple-element.3), channel_id=1, source_target_pairs={{0,30},{2,0},{4,2},{6,4},{8,6},{10,8},{12,10},{14,12},{16,14},{18,... | collective-permute-start | bytes 200 | tf_op jit(solution)/shard_map/ppermute | solution.py:9
  233.4 57.0 %collective-permute-start.28 = (bf16[512,512]{1,0:T(8,128)(2,1)S(1)}, bf16[512,512]{1,0:T(8,128)(2,1)S(1)}, u32[]{:S(2)}, u32[]{:S(2)}) collective-permute-start(bf16[512,512]{1,0:T(8,128)(2,1)S(1)} %collective-permute-done.24), channel_id=1, source_target_pairs={{0,30},{2,0},{4,2},{6,4},{8,6},{10,8},{12,10},{14,12},{16,14},{18,... | collective-permute-start | bytes 1572872 | tf_op jit(solution)/shard_map/ppermute | solution.py:9
  235.3 58.3 %collective-permute-start.30 = (bf16[512,512]{1,0:T(8,128)(2,1)S(1)}, bf16[512,512]{1,0:T(8,128)(2,1)S(1)}, u32[]{:S(2)}, u32[]{:S(2)}) collective-permute-start(bf16[512,512]{1,0:T(8,128)(2,1)S(1)} %collective-permute-done.26), channel_id=1, source_target_pairs={{0,480},{32,0},{64,32},{96,64},{128,96},{160,128},{192,160},{224,1... | collective-permute-start | bytes 1572872 | tf_op jit(solution)/shard_map/ppermute | solution.py:9
  237.4 9.0 %collective-permute-start.19 = (s32[4,4]{1,0:T(4,128)S(1)}, s32[4,4]{1,0:T(4,128)S(1)}, u32[]{:S(2)}, u32[]{:S(2)}) collective-permute-start(s32[4,4]{1,0:T(4,128)S(1)} %get-tuple-element.5), channel_id=1, source_target_pairs={{0,480},{32,0},{64,32},{96,64},{128,96},{160,128},{192,160},{224,1... | collective-permute-start | bytes 200 | tf_op jit(solution)/shard_map/ppermute | solution.py:9
  240.2 10.4 %collective-permute-start.21 = (s32[4,4]{1,0:T(4,128)S(1)}, s32[4,4]{1,0:T(4,128)S(1)}, u32[]{:S(2)}, u32[]{:S(2)}) collective-permute-start(s32[4,4]{1,0:T(4,128)S(1)} %collective-permute-done.17), channel_id=1, source_target_pairs={{0,30},{2,0},{4,2},{6,4},{8,6},{10,8},{12,10},{14,12},{16,14},{18,... | collective-permute-start | bytes 200 | tf_op jit(solution)/shard_map/ppermute | solution.py:9
  246.4 7.4 %collective-permute-start.23 = (s32[4,4]{1,0:T(4,128)S(1)}, s32[4,4]{1,0:T(4,128)S(1)}, u32[]{:S(2)}, u32[]{:S(2)}) collective-permute-start(s32[4,4]{1,0:T(4,128)S(1)} %collective-permute-done.19), channel_id=1, source_target_pairs={{0,480},{32,0},{64,32},{96,64},{128,96},{160,128},{192,160},{224,1... | collective-permute-start | bytes 200 | tf_op jit(solution)/shard_map/ppermute | solution.py:9
  250.6 7.6 %collective-permute-start.25 = (s32[4,4]{1,0:T(4,128)S(1)}, s32[4,4]{1,0:T(4,128)S(1)}, u32[]{:S(2)}, u32[]{:S(2)}) collective-permute-start(s32[4,4]{1,0:T(4,128)S(1)} %collective-permute-done.21), channel_id=1, source_target_pairs={{0,30},{2,0},{4,2},{6,4},{8,6},{10,8},{12,10},{14,12},{16,14},{18,... | collective-permute-start | bytes 200 | tf_op jit(solution)/shard_map/ppermute | solution.py:9
  253.8 7.6 %collective-permute-start.27 = (s32[4,4]{1,0:T(4,128)S(1)}, s32[4,4]{1,0:T(4,128)S(1)}, u32[]{:S(2)}, u32[]{:S(2)}) collective-permute-start(s32[4,4]{1,0:T(4,128)S(1)} %collective-permute-done.23), channel_id=1, source_target_pairs={{0,480},{32,0},{64,32},{96,64},{128,96},{160,128},{192,160},{224,1... | collective-permute-start | bytes 200 | tf_op jit(solution)/shard_map/ppermute | solution.py:9
  258.3 7.6 %collective-permute-start.29 = (s32[4,4]{1,0:T(4,128)S(1)}, s32[4,4]{1,0:T(4,128)S(1)}, u32[]{:S(2)}, u32[]{:S(2)}) collective-permute-start(s32[4,4]{1,0:T(4,128)S(1)} %collective-permute-done.25), channel_id=1, source_target_pairs={{0,30},{2,0},{4,2},{6,4},{8,6},{10,8},{12,10},{14,12},{16,14},{18,... | collective-permute-start | bytes 200 | tf_op jit(solution)/shard_map/ppermute | solution.py:9
  261.4 7.6 %collective-permute-start.31 = (s32[4,4]{1,0:T(4,128)S(1)}, s32[4,4]{1,0:T(4,128)S(1)}, u32[]{:S(2)}, u32[]{:S(2)}) collective-permute-start(s32[4,4]{1,0:T(4,128)S(1)} %collective-permute-done.27), channel_id=1, source_target_pairs={{0,480},{32,0},{64,32},{96,64},{128,96},{160,128},{192,160},{224,1... | collective-permute-start | bytes 200 | tf_op jit(solution)/shard_map/ppermute | solution.py:9
  265.9 7.6 %collective-permute-start.33 = (s32[4,4]{1,0:T(4,128)S(1)}, s32[4,4]{1,0:T(4,128)S(1)}, u32[]{:S(2)}, u32[]{:S(2)}) collective-permute-start(s32[4,4]{1,0:T(4,128)S(1)} %collective-permute-done.29), channel_id=1, source_target_pairs={{0,30},{2,0},{4,2},{6,4},{8,6},{10,8},{12,10},{14,12},{16,14},{18,... | collective-permute-start | bytes 200 | tf_op jit(solution)/shard_map/ppermute | solution.py:9
  269.1 7.6 %collective-permute-start.35 = (s32[4,4]{1,0:T(4,128)S(1)}, s32[4,4]{1,0:T(4,128)S(1)}, u32[]{:S(2)}, u32[]{:S(2)}) collective-permute-start(s32[4,4]{1,0:T(4,128)S(1)} %collective-permute-done.31), channel_id=1, source_target_pairs={{0,480},{32,0},{64,32},{96,64},{128,96},{160,128},{192,160},{224,1... | collective-permute-start | bytes 200 | tf_op jit(solution)/shard_map/ppermute | solution.py:9
  273.6 7.6 %collective-permute-start.37 = (s32[4,4]{1,0:T(4,128)S(1)}, s32[4,4]{1,0:T(4,128)S(1)}, u32[]{:S(2)}, u32[]{:S(2)}) collective-permute-start(s32[4,4]{1,0:T(4,128)S(1)} %collective-permute-done.33), channel_id=1, source_target_pairs={{0,30},{2,0},{4,2},{6,4},{8,6},{10,8},{12,10},{14,12},{16,14},{18,... | collective-permute-start | bytes 200 | tf_op jit(solution)/shard_map/ppermute | solution.py:9
  276.7 7.6 %collective-permute-start.39 = (s32[4,4]{1,0:T(4,128)S(1)}, s32[4,4]{1,0:T(4,128)S(1)}, u32[]{:S(2)}, u32[]{:S(2)}) collective-permute-start(s32[4,4]{1,0:T(4,128)S(1)} %collective-permute-done.35), channel_id=1, source_target_pairs={{0,480},{32,0},{64,32},{96,64},{128,96},{160,128},{192,160},{224,1... | collective-permute-start | bytes 200 | tf_op jit(solution)/shard_map/ppermute | solution.py:9
  281.2 7.6 %collective-permute-start.41 = (s32[4,4]{1,0:T(4,128)S(1)}, s32[4,4]{1,0:T(4,128)S(1)}, u32[]{:S(2)}, u32[]{:S(2)}) collective-permute-start(s32[4,4]{1,0:T(4,128)S(1)} %collective-permute-done.37), channel_id=1, source_target_pairs={{0,30},{2,0},{4,2},{6,4},{8,6},{10,8},{12,10},{14,12},{16,14},{18,... | collective-permute-start | bytes 200 | tf_op jit(solution)/shard_map/ppermute | solution.py:9
  284.4 5.2 collective-permute-start.43
  290.4 11.9 %collective-permute-start.32 = (bf16[512,512]{1,0:T(8,128)(2,1)S(1)}, bf16[512,512]{1,0:T(8,128)(2,1)S(1)}, u32[]{:S(2)}, u32[]{:S(2)}) collective-permute-start(bf16[512,512]{1,0:T(8,128)(2,1)S(1)} %collective-permute-done.28), channel_id=1, source_target_pairs={{0,30},{2,0},{4,2},{6,4},{8,6},{10,8},{12,10},{14,12},{16,14},{18,... | collective-permute-start | bytes 1572872 | tf_op jit(solution)/shard_map/ppermute | solution.py:9
  293.6 13.1 %collective-permute-start.34 = (bf16[512,512]{1,0:T(8,128)(2,1)S(1)}, bf16[512,512]{1,0:T(8,128)(2,1)S(1)}, u32[]{:S(2)}, u32[]{:S(2)}) collective-permute-start(bf16[512,512]{1,0:T(8,128)(2,1)S(1)} %collective-permute-done.30), channel_id=1, source_target_pairs={{0,480},{32,0},{64,32},{96,64},{128,96},{160,128},{192,160},{224,1... | collective-permute-start | bytes 1572872 | tf_op jit(solution)/shard_map/ppermute | solution.py:9
  302.3 14.3 %collective-permute-start.36 = (bf16[512,512]{1,0:T(8,128)(2,1)S(1)}, bf16[512,512]{1,0:T(8,128)(2,1)S(1)}, u32[]{:S(2)}, u32[]{:S(2)}) collective-permute-start(bf16[512,512]{1,0:T(8,128)(2,1)S(1)} %collective-permute-done.32), channel_id=1, source_target_pairs={{0,30},{2,0},{4,2},{6,4},{8,6},{10,8},{12,10},{14,12},{16,14},{18,... | collective-permute-start | bytes 1572872 | tf_op jit(solution)/shard_map/ppermute | solution.py:9
  306.7 17.6 %collective-permute-start.38 = (bf16[512,512]{1,0:T(8,128)(2,1)S(1)}, bf16[512,512]{1,0:T(8,128)(2,1)S(1)}, u32[]{:S(2)}, u32[]{:S(2)}) collective-permute-start(bf16[512,512]{1,0:T(8,128)(2,1)S(1)} %collective-permute-done.34), channel_id=1, source_target_pairs={{0,480},{32,0},{64,32},{96,64},{128,96},{160,128},{192,160},{224,1... | collective-permute-start | bytes 1572872 | tf_op jit(solution)/shard_map/ppermute | solution.py:9
  316.6 16.9 %collective-permute-start.40 = (bf16[512,512]{1,0:T(8,128)(2,1)S(1)}, bf16[512,512]{1,0:T(8,128)(2,1)S(1)}, u32[]{:S(2)}, u32[]{:S(2)}) collective-permute-start(bf16[512,512]{1,0:T(8,128)(2,1)S(1)} %collective-permute-done.36), channel_id=1, source_target_pairs={{0,30},{2,0},{4,2},{6,4},{8,6},{10,8},{12,10},{14,12},{16,14},{18,... | collective-permute-start | bytes 1572872 | tf_op jit(solution)/shard_map/ppermute | solution.py:9
  324.3 17.0 %collective-permute-start.42 = (bf16[512,512]{1,0:T(8,128)(2,1)S(1)}, bf16[512,512]{1,0:T(8,128)(2,1)S(1)}, u32[]{:S(2)}, u32[]{:S(2)}) collective-permute-start(bf16[512,512]{1,0:T(8,128)(2,1)S(1)} %collective-permute-done.38), channel_id=1, source_target_pairs={{0,480},{32,0},{64,32},{96,64},{128,96},{160,128},{192,160},{224,1... | collective-permute-start | bytes 1572872 | tf_op jit(solution)/shard_map/ppermute | solution.py:9
Sparse Core Ops, SparseCore 0:
  343.2 55.5 all-reduce.1
where the time goes:
time: 518 us; the launch traced here: 516 us
  starting transfers between devices  213 us (41%)
  waiting for transfers between devices  168 us (32%)
  blocking collectives  105 us (20%)
  between operations  16.8 us (3%)
    ppermute x44, starting transfers between devices, from_behind(): lax.ppermute(value, axis, [(i, (i + by) % size) for i in range(size)])  213 us
    ppermute x44, waiting for transfers between devices, from_behind(): lax.ppermute(value, axis, [(i, (i + by) % size) for i in range(size)])  112 us
    psum x1, blocking collectives, per_device(): squares = lax.psum(jnp.sum(part_sum * part_sum), ('row', 'col', 'depth'))  105 us
    psum x1, waiting for transfers between devices, per_device(): whole_sum = lax.psum(total, 'depth')  55.7 us
  transfers between devices with their start and end apart: 45, of which 15 were waited for; matrix products, arithmetic and copies ran while one was open for 1% of the time, Pallas kernels for 0%

commit v1 on v0

v1 whole, which is shorter than its diff:
```python
import functools

import jax
import jax.numpy as jnp
from jax import lax
from jax.experimental import pallas as pl
from jax.experimental.pallas import tpu as pltpu
from jax.sharding import PartitionSpec as P


def apply_mask(panel, mask):
    blocks_r, blocks_c = mask.shape
    size_r = panel.shape[0] // blocks_r
    size_c = panel.shape[1] // blocks_c
    spread = jnp.repeat(jnp.repeat(mask, size_r, 0), size_c, 1)
    return jnp.where(spread != 0, panel, jnp.zeros_like(panel))


def product_kernel(a_ref, b_ref, mine_ref, theirs_ref):
    step = pl.program_id(0)
    half = mine_ref.shape[1]
    part = jnp.dot(a_ref[0], b_ref[0], preferred_element_type=jnp.float32)

    @pl.when(step == 0)
    def _():
        mine_ref[...] = part[:, :half]
        theirs_ref[...] = part[:, half:]

    @pl.when(step > 0)
    def _():
        mine_ref[...] += part[:, :half]
        theirs_ref[...] += part[:, half:]


def multiply(a_all, b_all):
    count, rows, depth = a_all.shape
    cols = b_all.shape[2]
    half = jax.ShapeDtypeStruct((rows, cols // 2), jnp.float32)
    spec = pl.BlockSpec((rows, cols // 2), lambda s: (0, 0))
    return pl.pallas_call(
        product_kernel,
        grid=(count,),
        in_specs=[
            pl.BlockSpec((1, rows, depth), lambda s: (s, 0, 0)),
            pl.BlockSpec((1, depth, cols), lambda s: (s, 0, 0)),
        ],
        out_specs=[spec, spec],
        out_shape=[half, half],
        compiler_params=pltpu.CompilerParams(vmem_limit_bytes=24 << 20),
        cost_estimate=pl.CostEstimate(
            flops=2 * count * rows * depth * cols,
            bytes_accessed=a_all.size * 2 + b_all.size * 2 + rows * cols * 4,
            transcendentals=0,
        ),
    )(a_all, b_all)


def per_device(a_matrix, b_matrix, mask_a, mask_b):
    layer = lax.axis_index("depth")
    layers = lax.axis_size("depth")
    count = lax.axis_size("row")
    width = a_matrix.shape[0]
    share = width // layers
    masked_a = apply_mask(a_matrix, mask_a)
    masked_b = apply_mask(b_matrix, mask_b)
    a_part = lax.dynamic_slice_in_dim(masked_a, layer * share, share, 1)
    b_part = lax.dynamic_slice_in_dim(masked_b, layer * share, share, 0)
    b_part = jnp.where(
        layer == 0, b_part, jnp.concatenate([b_part[:, share:], b_part[:, :share]], 1)
    )
    a_all = lax.all_gather(a_part, "col", axis=0)
    b_all = lax.all_gather(b_part, "row", axis=0)
    mine, theirs = multiply(a_all, b_all)
    other = lax.ppermute(theirs, "depth", [(0, 1), (1, 0)])
    full = mine + other
    squares = lax.psum(jnp.sum(full * full), ("row", "col", "depth"))
    entries = float(width * count * (width * count))
    rms_norm = jnp.sqrt(squares / entries + 1e-06)
    return (full.astype(jnp.bfloat16), rms_norm)


def solution(mesh):
    placed = (P("row", "col"), P("row", "col"), P("row", "col"), P("row", "col"))
    return jax.shard_map(
        per_device,
        mesh=mesh,
        in_specs=placed,
        out_specs=(P("row", ("col", "depth")), P()),
        check_vma=False,
    )
```

time: 518 us -> 291 us (0.56)
  starting transfers between devices: 213 us -> 2.66 us
  waiting for transfers between devices: 168 us -> 148 us
  Pallas kernels: 0 us -> 6.32 us
    ppermute x44 -> x1, starting transfers between devices: 213 us -> 2.58 us  [per_device(): other = lax.ppermute(theirs, 'depth', [(0, 1), (1, 0)])]
    all_gather x0 -> x2, waiting for transfers between devices: none -> 146 us  [the longest x1 75.2 us: per_device(): b_all = lax.all_gather(b_part, 'row', axis=0)]
    ppermute x44 -> x1, waiting for transfers between devices: 112 us -> 1.51 us  [per_device(): other = lax.ppermute(theirs, 'depth', [(0, 1), (1, 0)])]
    psum x1 -> x0, waiting for transfers between devices: 55.7 us -> none  [per_device(): whole_sum = lax.psum(total, 'depth')]
    pallas_call x0 -> x1, Pallas kernels: none -> 6.32 us  [multiply(): pl.pallas_call(product_kernel, grid=(count,), in_specs=[pl.BlockSpec((1,...]
  transfers between devices with their start and end apart: 45 -> 3, of which waited for: 15 -> 3; matrix products, arithmetic and copies ran while one was open for 1% -> 1% of each run, Pallas kernels for 0% -> 0%
where the time goes in v1:
time: 291 us
  waiting for transfers between devices  148 us (51%)
  blocking collectives  104 us (36%)
  between operations  15.9 us (5%)
  local copies, waits for them, and re-layouts  7.91 us (3%)
  other arithmetic  6.32 us (2%)
  Pallas kernels  6.32 us (2%)
    psum x1, blocking collectives, per_device(): squares = lax.psum(jnp.sum(full * full), ('row', 'col', 'depth'))  104 us
    all_gather x1, waiting for transfers between devices, per_device(): b_all = lax.all_gather(b_part, 'row', axis=0)  75.2 us
    all_gather x1, waiting for transfers between devices, per_device(): a_all = lax.all_gather(a_part, 'col', axis=0)  71 us
    pallas_call x1, Pallas kernels, multiply(): pl.pallas_call(product_kernel, grid=(count,), in_specs=[pl.BlockSpec((1,...  6.32 us
  transfers between devices with their start and end apart: 3, of which 3 were waited for; matrix products, arithmetic and copies ran while one was open for 1% of the time, Pallas kernels for 0%

profile of v1, /device:TPU:1, one launch (start us, length us, event | category | flops | bytes accessed | tf_op | source)
XLA Modules:
  0.0 290.9 jit_solution(1403995771274763014)
XLA Ops:
  7.2 0.0 all-gather.5.cloned.1.call-start
  7.2 0.7 broadcast_compare_fusion.1
  7.9 1.6 broadcast_in_dim.13
  9.5 0.1 copy.11
  9.7 1.7 dynamic-slice_select_fusion.1
  11.4 0.0 all-gather.5.cloned.1.call-update
  11.4 0.0 all-gather.7.cloned.1.call-start
  11.5 0.7 broadcast_compare_fusion
  12.2 1.6 broadcast_in_dim.15
  13.8 0.1 copy.10
  14.0 1.0 dynamic-slice_select_fusion
  15.0 0.8 maximum_select_fusion
  15.8 0.0 all-gather.7.cloned.1.call-update
  15.8 71.0 %all-gather.5.cloned.1.call-done = bf16[8192,256]{1,0:T(8,128)(2,1)} async-done(((bf16[512,256]{1,0:T(8,128)(2,1)}), bf16[8192,256]{1,0:T(8,128)(2,1)}) %all-gather.5.cloned.1.call-update) | async-done | bytes 4194320 | tf_op jit(solution)/shard_map/all_gather | solution.py:71
  86.8 75.2 %all-gather.7.cloned.1.call-done = bf16[4096,512]{1,0:T(8,128)(2,1)} async-done(((bf16[256,512]{1,0:T(8,128)(2,1)}), bf16[4096,512]{1,0:T(8,128)(2,1)}) %all-gather.7.cloned.1.call-update) | async-done | bytes 4194320 | tf_op jit(solution)/shard_map/all_gather | solution.py:72
  162.1 0.0 copy-start
  162.1 2.2 copy-done
  164.3 0.0 copy-start.1
  164.3 2.2 copy-done.1
  166.4 6.3 %shard_map.59 = (f32[512,256]{1,0:T(8,128)S(1)}, f32[512,256]{1,0:T(8,128)S(1)}) custom-call(bf16[16,512,256]{2,1,0:T(8,128)(2,1)S(1)} %bitcast.12, bf16[16,256,512]{2,1,0:T(8,128)(2,1)S(1)} %bitcast.13), custom_call_target="tpu_custom_call" | custom-call | flops 2147483648 | bytes 9437184 | tf_op jit(solution)/shard_map/pallas_call | solution.py:40
  172.8 2.6 collective-permute-start
  175.4 1.5 collective-permute-done
  176.9 1.4 multiply_reduce_fusion
  178.3 104.0 %psum.7 = f32[]{:T(128)} all-reduce(f32[]{:T(128)} %get-tuple-element.6), channel_id=1, replica_groups=mesh['row'=16,'col'=16,'depth'=2] {'row','col','depth'}, use_global_device_ids=true, to_apply=%region_1.2 | all-reduce | flops 1 | bytes 8 | tf_op jit(solution)/shard_map/psum | solution.py:76
  (3 shorter events, 0.1 us)
Async XLA Ops:
  7.2 79.7 %all-gather.5.cloned.1.call-start = ((), (), s32[]{:S(2)}) async-start(), calls=%async_computation | async-start | bytes 4456448 | tf_op jit(solution)/shard_map/all_gather | solution.py:71
  11.4 150.6 %all-gather.7.cloned.1.call-start = ((), (), s32[]{:S(2)}) async-start(), calls=%async_computation.1 | async-start | bytes 4456448 | tf_op jit(solution)/shard_map/all_gather | solution.py:72
  162.1 2.2 copy-start
  164.3 2.2 copy-start.1
  172.8 4.1 %collective-permute-start = (f32[512,256]{1,0:T(8,128)S(1)}, f32[512,256]{1,0:T(8,128)S(1)}, u32[]{:S(2)}, u32[]{:S(2)}) collective-permute-start(f32[512,256]{1,0:T(8,128)S(1)} %get-tuple-element.5), channel_id=1, source_target_pairs={{0,1},{1,0},{2,3},{3,2},{4,5},{5,4},{6,7},{7,6},{8,9},{9,8},{10,11... | collective-permute-start | bytes 1572872 | tf_op jit(solution)/shard_map/ppermute | solution.py:74
Sparse Core Ops, SparseCore 0:
  11.6 75.2 all-gather.4
  89.8 72.1 all-gather.6

commit v2 on v1

v2 whole, which is shorter than its diff:
```python
import jax
import jax.numpy as jnp
from jax import lax
from jax.experimental import pallas as pl
from jax.experimental.pallas import tpu as pltpu
from jax.sharding import PartitionSpec as P


def mask_kernel(layer_ref, mask_a_ref, mask_b_ref, a_ref, b_ref, a_out, b_out):
    layer = layer_ref[0]
    blocks = mask_a_ref.shape[0]
    size = a_ref.shape[0] // blocks
    half = blocks // 2
    share = half * size
    for d in range(2):
        @pl.when(layer == d)
        def _(d=d):
            for i in range(blocks):
                for j in range(half):
                    k = d * half + j
                    tile = a_ref[i * size:(i + 1) * size, k * size:(k + 1) * size]
                    keep = mask_a_ref[i, k] != 0
                    a_out[i * size:(i + 1) * size, j * size:(j + 1) * size] = jnp.where(
                        keep, tile, jnp.zeros_like(tile)
                    )
                    c = (i * size + d * share) % (2 * share)
                    tile = b_ref[k * size:(k + 1) * size, i * size:(i + 1) * size]
                    keep = mask_b_ref[k, i] != 0
                    b_out[j * size:(j + 1) * size, c:c + size] = jnp.where(
                        keep, tile, jnp.zeros_like(tile)
                    )


def mask_parts(layer, mask_a, mask_b, a_matrix, b_matrix):
    width = a_matrix.shape[0]
    smem = pl.BlockSpec(memory_space=pltpu.SMEM)
    vmem = pl.BlockSpec(memory_space=pltpu.VMEM)
    return pl.pallas_call(
        mask_kernel,
        in_specs=[smem, smem, smem, vmem, vmem],
        out_specs=[vmem, vmem],
        out_shape=[
            jax.ShapeDtypeStruct((width, width // 2), a_matrix.dtype),
            jax.ShapeDtypeStruct((width // 2, width), b_matrix.dtype),
        ],
        compiler_params=pltpu.CompilerParams(vmem_limit_bytes=16 << 20),
    )(layer[None], mask_a, mask_b, a_matrix, b_matrix)


def product_kernel(a_ref, b_ref, mine_ref, theirs_ref):
    step = pl.program_id(0)
    half = mine_ref.shape[1]
    part = jnp.dot(a_ref[0], b_ref[0], preferred_element_type=jnp.float32)
    for s in range(1, a_ref.shape[0]):
        part += jnp.dot(a_ref[s], b_ref[s], preferred_element_type=jnp.float32)

    @pl.when(step == 0)
    def _():
        mine_ref[...] = part[:, :half]
        theirs_ref[...] = part[:, half:]

    @pl.when(step > 0)
    def _():
        mine_ref[...] += part[:, :half]
        theirs_ref[...] += part[:, half:]


def multiply(a_all, b_all, group=4):
    count, rows, depth = a_all.shape
    cols = b_all.shape[2]
    half = jax.ShapeDtypeStruct((rows, cols // 2), jnp.float32)
    spec = pl.BlockSpec((rows, cols // 2), lambda s: (0, 0))
    return pl.pallas_call(
        product_kernel,
        grid=(count // group,),
        in_specs=[
            pl.BlockSpec((group, rows, depth), lambda s: (s, 0, 0)),
            pl.BlockSpec((group, depth, cols), lambda s: (s, 0, 0)),
        ],
        out_specs=[spec, spec],
        out_shape=[half, half],
        compiler_params=pltpu.CompilerParams(vmem_limit_bytes=56 << 20),
        cost_estimate=pl.CostEstimate(
            flops=2 * count * rows * depth * cols,
            bytes_accessed=a_all.size * 2 + b_all.size * 2 + rows * cols * 4,
            transcendentals=0,
        ),
    )(a_all, b_all)


def total_over(value, axis, size):
    copies = jnp.broadcast_to(value, (size,) + value.shape)
    return jnp.sum(lax.all_to_all(copies, axis, 0, 0, tiled=True), 0)


def per_device(a_matrix, b_matrix, mask_a, mask_b):
    layer = lax.axis_index("depth")
    layers = lax.axis_size("depth")
    count = lax.axis_size("row")
    width = a_matrix.shape[0]
    a_part, b_part = mask_parts(layer, mask_a, mask_b, a_matrix, b_matrix)
    a_all = lax.all_gather(a_part, "col", axis=0)
    copies = jnp.broadcast_to(b_part, (count,) + b_part.shape)
    b_all = lax.all_to_all(copies, "row", 0, 0, tiled=True)
    mine, theirs = multiply(a_all, b_all)
    other = lax.ppermute(theirs, "depth", [(0, 1), (1, 0)])
    full = mine + other
    squares = jnp.sum(jnp.square(full).reshape(-1, 1, 128), 0)
    squares = total_over(squares, ("row", "depth"), count * layers)
    near = [[4 * g + i for i in range(4)] for g in range(count // 4)]
    far = [[4 * g + i for g in range(count // 4)] for i in range(4)]
    for groups in (near, far):
        squares = jnp.sum(lax.all_gather(squares, "col", axis_index_groups=groups), 0)
    entries = float(width * count * (width * count))
    rms_norm = jnp.sqrt(jnp.sum(squares) / entries + 1e-06)
    return (full.astype(jnp.bfloat16), rms_norm)


def solution(mesh):
    placed = (P("row", "col"), P("row", "col"), P("row", "col"), P("row", "col"))
    return jax.shard_map(
        per_device,
        mesh=mesh,
        in_specs=placed,
        out_specs=(P("row", ("col", "depth")), P()),
        check_vma=False,
    )
```

time: 291 us -> 154 us (0.53)
  waiting for transfers between devices: 148 us -> 21.1 us
  blocking collectives: 104 us -> 88.8 us
  starting transfers between devices: 2.66 us -> 10.8 us
  local copies, waits for them, and re-layouts: 7.91 us -> 3.88 us
  other arithmetic: 6.32 us -> 2.61 us
    psum x1 -> x0, blocking collectives: 104 us -> none  [per_device(): squares = lax.psum(jnp.sum(full * full), ('row', 'col', 'depth'))]
    all_gather x1 -> x0, waiting for transfers between devices: 75.2 us -> none  [per_device(): b_all = lax.all_gather(b_part, 'row', axis=0)]
    all_to_all x0 -> x2, blocking collectives: none -> 69.9 us  [the longest x1 56 us: per_device(): b_all = lax.all_to_all(copies, 'row', 0, 0, tiled=True)]
    all_gather x1, waiting for transfers between devices: 71 us -> 19.4 us  [per_device(): a_all = lax.all_gather(a_part, 'col', axis=0)]
    all_gather x0 -> x2, blocking collectives: none -> 18.9 us  [per_device(): lax.all_gather(squares, 'col', axis_index_groups=groups)]
    ppermute x1, starting transfers between devices: 2.58 us -> 10.8 us  [per_device(): other = lax.ppermute(theirs, 'depth', [(0, 1), (1, 0)])]
    select_n x3 -> x0, other arithmetic: 3.57 us -> none  [the longest x2 2.78 us: apply_mask(): return jnp.where(spread != 0, panel, jnp.zeros_like(panel))]
    pallas_call x1 -> x2, Pallas kernels: 6.32 us -> 8.14 us  [the longest x1 6.72 us: multiply(): pl.pallas_call(product_kernel, grid=(count // group,), in_specs=[pl.Block...]
  transfers between devices with their start and end apart: 3 -> 2, of which waited for: 3 -> 2; matrix products, arithmetic and copies ran while one was open for 1% -> 0% of each run, Pallas kernels for 0% -> 0%
where the time goes in v2:
time: 154 us; the launch traced here: 151 us
  blocking collectives  88.8 us (58%)
  waiting for transfers between devices  21.1 us (14%)
  between operations  15.9 us (10%)
  starting transfers between devices  10.8 us (7%)
  Pallas kernels  8.14 us (5%)
  local copies, waits for them, and re-layouts  3.88 us (3%)
  other arithmetic  2.61 us (2%)
    all_to_all x1, blocking collectives, per_device(): b_all = lax.all_to_all(copies, 'row', 0, 0, tiled=True)  56 us
    all_gather x1, waiting for transfers between devices, per_device(): a_all = lax.all_gather(a_part, 'col', axis=0)  19.4 us
    all_gather x2, blocking collectives, per_device(): lax.all_gather(squares, 'col', axis_index_groups=groups)  18.9 us
    all_to_all x1, blocking collectives, total_over(): return jnp.sum(lax.all_to_all(copies, axis, 0, 0, tiled=True), 0)  13.9 us
    ppermute x1, starting transfers between devices, per_device(): other = lax.ppermute(theirs, 'depth', [(0, 1), (1, 0)])  10.8 us
    pallas_call x1, Pallas kernels, multiply(): pl.pallas_call(product_kernel, grid=(count // group,), in_specs=[pl.Block...  6.72 us
    unnamed x8, local copies, waits for them, and re-layouts  3.44 us
  transfers between devices with their start and end apart: 2, of which 2 were waited for; matrix products, arithmetic and copies ran while one was open for 0% of the time, Pallas kernels for 0%

profile of v2, /device:TPU:1, one launch (start us, length us, event | category | flops | bytes accessed | tf_op | source)
XLA Modules:
  0.0 151.3 jit_solution(8417602588316473204)
XLA Ops:
  7.2 0.0 all-gather.7.cloned.1.call-start
  7.2 0.0 copy-start
  7.2 1.0 copy-done
  8.3 0.0 copy-start.1
  8.3 1.0 copy-done.1
  9.3 0.0 copy-start.2
  9.3 0.7 copy-done.2
  10.0 0.0 copy-start.3
  10.0 0.7 copy-done.3
  10.7 1.4 shard_map.59
  12.1 0.0 all-gather.7.cloned.1.call-update
  12.1 0.4 broadcast_in_dim.10
  12.5 56.0 %all_to_all.10.b_ref = bf16[16,256,512]{2,1,0:T(8,128)(2,1)} all-to-all(bf16[16,256,512]{2,1,0:T(8,128)(2,1)S(1)} %broadcast_in_dim.10), channel_id=1, replica_groups=mesh['row'=16,'col'=16,'depth'=2] {'row'}, dimensions={0} | all-to-all | bytes 8388608 | tf_op jit(solution)/shard_map/all_to_all | solution.py:104
  68.5 19.4 %all-gather.7.cloned.1.call-done = bf16[8192,256]{1,0:T(8,128)(2,1)} async-done(((bf16[512,256]{1,0:T(8,128)(2,1)}), bf16[8192,256]{1,0:T(8,128)(2,1)}) %all-gather.7.cloned.1.call-update) | async-done | bytes 4194320 | tf_op jit(solution)/shard_map/all_gather | solution.py:102
  87.9 6.7 %shard_map.60 = (f32[512,256]{1,0:T(8,128)}, f32[512,256]{1,0:T(8,128)}) custom-call(bf16[16,512,256]{2,1,0:T(8,128)(2,1)} %bitcast.5, bf16[16,256,512]{2,1,0:T(8,128)(2,1)} %all_to_all.10.b_ref), custom_call_target="tpu_custom_call" | custom-call | flops 2147483648 | bytes 9437184 | tf_op jit(solution)/shard_map/pallas_call | solution.py:73
  94.6 10.8 %collective-permute-start = (f32[512,256]{1,0:T(8,128)}, f32[512,256]{1,0:T(8,128)S(1)}, u32[]{:S(2)}, u32[]{:S(2)}) collective-permute-start(f32[512,256]{1,0:T(8,128)} %get-tuple-element.9), channel_id=1, source_target_pairs={{0,1},{1,0},{2,3},{3,2},{4,5},{5,4},{6,7},{7,6},{8,9},{9,8},{10,11... | collective-permute-start | bytes 1572872 | tf_op jit(solution)/shard_map/ppermute | solution.py:106
  105.4 1.7 %collective-permute-done = f32[512,256]{1,0:T(8,128)S(1)} collective-permute-done((f32[512,256]{1,0:T(8,128)}, f32[512,256]{1,0:T(8,128)S(1)}, u32[]{:S(2)}, u32[]{:S(2)}) %collective-permute-start) | collective-permute-done | bytes 524320 | tf_op jit(solution)/shard_map/ppermute | solution.py:106
  107.1 1.8 %add_multiply_fusion = (f32[512,256]{1,0:T(8,128)S(1)}, bf16[512,256]{1,0:T(8,128)(2,1)}) fusion(f32[512,256]{1,0:T(8,128)} %get-tuple-element.8, f32[512,256]{1,0:T(8,128)S(1)} %collective-permute-done), kind=kLoop, calls=%fused_computation | loop fusion | flops 393216 | bytes 1835008 | tf_op jit(solution)/shard_map/square | solution.py:108
  109.0 0.1 reduce_sum.40
  109.2 13.9 %all_to_all.11 = f32[32,1,128]{2,1,0:T(1,128)S(1)} all-to-all(f32[32,1,128]{2,1,0:T(1,128)S(1)} %broadcast_in_dim.11), channel_id=1, replica_groups=mesh['row'=16,'col'=16,'depth'=2] {'row','depth'}, dimensions={0} | all-to-all | bytes 32768 | tf_op jit(solution)/shard_map/all_to_all | solution.py:93
  123.1 8.1 %all-gather.3 = f32[4,1,128]{2,1,0:T(1,128)S(1)} all-gather(f32[1,1,128]{2,1,0:T(1,128)S(1)} %bitcast.7), channel_id=3, replica_groups={{0,2,4,6},{8,10,12,14},{16,18,20,22},{24,26,28,30},{1,3,5,7},{9,11,13,1..., dimensions={0}, use_global_device_ids=true | all-gather | bytes 2560 | tf_op jit(solution)/shard_map/all_gather | solution.py:113
  131.2 10.8 %all-gather.4 = f32[4,1,128]{2,1,0:T(1,128)S(1)} all-gather(f32[1,1,128]{2,1,0:T(1,128)S(1)} %bitcast.8), channel_id=4, replica_groups={{0,8,16,24},{2,10,18,26},{4,12,20,28},{6,14,22,30},{1,9,17,25},{3,11,19..., dimensions={0}, use_global_device_ids=true | all-gather | bytes 2560 | tf_op jit(solution)/shard_map/all_gather | solution.py:113
  142.0 0.6 reduce.5
  (4 shorter events, 0.1 us)
Async XLA Ops:
  7.2 80.7 %all-gather.7.cloned.1.call-start = ((), (), s32[]{:S(2)}) async-start(), calls=%async_computation.2 | async-start | bytes 4456448 | tf_op jit(solution)/shard_map/all_gather | solution.py:102
  7.2 1.0 copy-start
  8.3 1.0 copy-start.1
  9.3 0.7 copy-start.2
  10.0 0.7 copy-start.3
  94.6 12.5 %collective-permute-start = (f32[512,256]{1,0:T(8,128)}, f32[512,256]{1,0:T(8,128)S(1)}, u32[]{:S(2)}, u32[]{:S(2)}) collective-permute-start(f32[512,256]{1,0:T(8,128)} %get-tuple-element.9), channel_id=1, source_target_pairs={{0,1},{1,0},{2,3},{3,2},{4,5},{5,4},{6,7},{7,6},{8,9},{9,8},{10,11... | collective-permute-start | bytes 1572872 | tf_op jit(solution)/shard_map/ppermute | solution.py:106
Sparse Core Ops, SparseCore 0:
  12.2 75.6 all-gather.6

commit v3 on v2

v3 whole, which is shorter than its diff:
```python
import jax
import jax.numpy as jnp
from jax import lax
from jax.experimental import pallas as pl
from jax.experimental.pallas import tpu as pltpu
from jax.sharding import PartitionSpec as P


def mask_kernel(layer_ref, mask_ref, matrix_ref, out_ref):
    blocks = mask_ref.shape[0]
    size = matrix_ref.shape[0] // blocks
    half = blocks // 2
    layer = layer_ref[0]
    for d in range(2):
        @pl.when(layer == d)
        def _(d=d):
            for i in range(blocks):
                for j in range(half):
                    k = d * half + j
                    tile = matrix_ref[i * size:(i + 1) * size, k * size:(k + 1) * size]
                    out_ref[i * size:(i + 1) * size, j * size:(j + 1) * size] = jnp.where(
                        mask_ref[i, k] != 0, tile, jnp.zeros_like(tile)
                    )


def masked_half(layer, mask, matrix):
    width = matrix.shape[0]
    smem = pl.BlockSpec(memory_space=pltpu.SMEM)
    vmem = pl.BlockSpec(memory_space=pltpu.VMEM)
    return pl.pallas_call(
        mask_kernel,
        in_specs=[smem, smem, vmem],
        out_specs=vmem,
        out_shape=jax.ShapeDtypeStruct((width, width // 2), matrix.dtype),
        compiler_params=pltpu.CompilerParams(vmem_limit_bytes=58 << 20),
        cost_estimate=pl.CostEstimate(
            flops=0, bytes_accessed=matrix.size * 3, transcendentals=0
        ),
    )(layer[None], mask, matrix)


def total_over(value, axis, size):
    copies = jnp.broadcast_to(value, (size,) + value.shape)
    return jnp.sum(lax.all_to_all(copies, axis, 0, 0, tiled=True), 0)


def per_device(a_matrix, b_matrix, mask_a, mask_b):
    layer = lax.axis_index("depth")
    layers = lax.axis_size("depth")
    count = lax.axis_size("row")
    width = a_matrix.shape[0]
    share = width // layers
    a_part = masked_half(layer, mask_a, a_matrix)
    a_all = lax.all_gather(a_part, ("col", "depth"), axis=0)
    b_part = masked_half(layer, mask_b, b_matrix)
    copies = jnp.broadcast_to(b_part, (count,) + b_part.shape)
    b_all = lax.all_to_all(copies, "row", 0, 0, tiled=True)
    b_all = b_all.reshape(count * layers, share, share)
    full = jnp.einsum("smk,skn->mn", a_all, b_all, preferred_element_type=jnp.float32)
    squares = jnp.sum(jnp.square(full).reshape(-1, 1, 128), 0)
    squares = total_over(squares, ("row", "depth"), count * layers)
    near = [[4 * g + i for i in range(4)] for g in range(count // 4)]
    far = [[4 * g + i for g in range(count // 4)] for i in range(4)]
    for groups in (near, far):
        squares = jnp.sum(lax.all_gather(squares, "col", axis_index_groups=groups), 0)
    entries = float(width * count * (width * count))
    rms_norm = jnp.sqrt(jnp.sum(squares) / entries + 1e-06)
    return (full.astype(jnp.bfloat16), rms_norm)


def solution(mesh):
    placed = (P("row", "col"), P("row", "col"), P("row", "col"), P("row", "col"))
    return jax.shard_map(
        per_device,
        mesh=mesh,
        in_specs=placed,
        out_specs=(P("row", ("col", "depth")), P()),
        check_vma=False,
    )
```

time: 154 us -> 148 us (0.961)
  starting transfers between devices: 10.8 us -> 0.04 us
  matrix products: 0 us -> 7.6 us
  waiting for transfers between devices: 21.1 us -> 27.4 us
  Pallas kernels: 8.14 us -> 3.65 us
  local copies, waits for them, and re-layouts: 3.88 us -> 1.39 us
  other arithmetic: 2.61 us -> 0.8 us
    ppermute x1 -> x0, starting transfers between devices: 10.8 us -> none  [per_device(): other = lax.ppermute(theirs, 'depth', [(0, 1), (1, 0)])]
    all_gather x1, waiting for transfers between devices: 19.4 us -> 27.4 us  [per_device(): a_all = lax.all_gather(a_part, ('col', 'depth'), axis=0)]
    dot_general x0 -> x1, matrix products: none -> 7.6 us  [per_device(): jnp.einsum('smk,skn->mn', a_all, b_all, preferred_element_type=jnp.float32)]
    pallas_call x2, Pallas kernels: 8.14 us -> 3.65 us  [masked_half(): pl.pallas_call(mask_kernel, in_specs=[smem, smem, vmem], out_specs=vmem,...]
    unnamed x8 -> x0, local copies, waits for them, and re-layouts: 3.44 us -> none
    square x1 -> x0, other arithmetic: 1.82 us -> none  [per_device(): squares = jnp.sum(jnp.square(full).reshape(-1, 1, 128), 0)]
    ppermute x1 -> x0, waiting for transfers between devices: 1.73 us -> none  [per_device(): other = lax.ppermute(theirs, 'depth', [(0, 1), (1, 0)])]
  transfers between devices with their start and end apart: 2 -> 1, of which waited for: 2 -> 1; matrix products, arithmetic and copies ran while one was open for 0% -> 1% of each run, Pallas kernels for 0% -> 1%
where the time goes in v3:
time: 148 us; the launch traced here: 146 us
  blocking collectives  89.1 us (60%)
  waiting for transfers between devices  27.4 us (19%)
  between operations  15.9 us (11%)
  matrix products  7.6 us (5%)
  Pallas kernels  3.65 us (2%)
    all_to_all x1, blocking collectives, per_device(): b_all = lax.all_to_all(copies, 'row', 0, 0, tiled=True)  56 us
    all_gather x1, waiting for transfers between devices, per_device(): a_all = lax.all_gather(a_part, ('col', 'depth'), axis=0)  27.4 us
    all_gather x2, blocking collectives, per_device(): lax.all_gather(squares, 'col', axis_index_groups=groups)  19.1 us
    all_to_all x1, blocking collectives, total_over(): return jnp.sum(lax.all_to_all(copies, axis, 0, 0, tiled=True), 0)  14 us
    dot_general x1, matrix products, per_device(): jnp.einsum('smk,skn->mn', a_all, b_all, preferred_element_type=jnp.float32)  7.6 us
    pallas_call x2, Pallas kernels, masked_half(): pl.pallas_call(mask_kernel, in_specs=[smem, smem, vmem], out_specs=vmem,...  3.65 us
  transfers between devices with their start and end apart: 1, of which 1 were waited for; matrix products, arithmetic and copies ran while one was open for 1% of the time, Pallas kernels for 1%

profile of v3, /device:TPU:1, one launch (start us, length us, event | category | flops | bytes accessed | tf_op | source)
XLA Modules:
  0.0 145.9 jit_solution(16737291453875623301)
XLA Ops:
  7.2 0.0 all-gather.7.cloned.1.call-start
  7.2 1.8 %shard_map.59 = bf16[512,256]{1,0:T(8,128)(2,1)} custom-call(s32[1]{0:T(128)} %bitcast.layer_ref, s32[4,4]{1,0:T(4,128)} %mask_ref.2, bf16[512,512]{1,0:T(8,128)(2,1)} %matrix_ref.2), custom_call_target="tpu_custom_call" | custom-call | bytes 786432 | tf_op jit(solution)/shard_map/pallas_call | solution.py:30
  9.0 0.0 all-gather.7.cloned.1.call-update
  9.1 1.8 %shard_map.60 = bf16[512,256]{1,0:T(8,128)(2,1)} custom-call(s32[1]{0:T(128)} %bitcast.layer_ref, s32[4,4]{1,0:T(4,128)} %mask_ref.3, bf16[512,512]{1,0:T(8,128)(2,1)} %matrix_ref.3), custom_call_target="tpu_custom_call" | custom-call | bytes 786432 | tf_op jit(solution)/shard_map/pallas_call | solution.py:30
  10.9 1.3 broadcast_in_dim.11
  12.2 56.0 %all_to_all.10 = bf16[16,512,256]{2,1,0:T(8,128)(2,1)} all-to-all(bf16[16,512,256]{2,1,0:T(8,128)(2,1)S(1)} %broadcast_in_dim.11), channel_id=1, replica_groups=mesh['row'=16,'col'=16,'depth'=2] {'row'}, dimensions={0} | all-to-all | bytes 8388608 | tf_op jit(solution)/shard_map/all_to_all | solution.py:57
  68.2 27.4 %all-gather.7.cloned.1.call-done = bf16[16384,256]{1,0:T(8,128)(2,1)} async-done(((bf16[512,256]{1,0:T(8,128)(2,1)}), bf16[16384,256]{1,0:T(8,128)(2,1)}) %all-gather.7.cloned.1.call-update) | async-done | bytes 8388624 | tf_op jit(solution)/shard_map/all_gather | solution.py:54
  95.6 7.6 %fusion = (bf16[512,256]{1,0:T(8,128)(2,1)}, f32[512,256]{1,0:T(8,128)S(1)}) fusion(bf16[32,512,256]{2,1,0:T(8,128)(2,1)} %bitcast.14, bf16[32,256,256]{2,1,0:T(8,128)(2,1)} %bitcast.10), kind=kOutput, calls=%fused_computation.1 | convolution fusion | flops 2147745792 | bytes 13369344 | tf_op jit(solution)/shard_map/smk,skn->mn/dot_general | solution.py:59
  103.3 0.1 reduce_sum.40
  103.4 14.0 %all_to_all.11 = f32[32,1,128]{2,1,0:T(1,128)S(1)} all-to-all(f32[32,1,128]{2,1,0:T(1,128)S(1)} %broadcast_in_dim.12), channel_id=1, replica_groups=mesh['row'=16,'col'=16,'depth'=2] {'row','depth'}, dimensions={0} | all-to-all | bytes 32768 | tf_op jit(solution)/shard_map/all_to_all | solution.py:44
  117.5 8.0 %all-gather.3 = f32[4,1,128]{2,1,0:T(1,128)S(1)} all-gather(f32[1,1,128]{2,1,0:T(1,128)S(1)} %bitcast.12), channel_id=3, replica_groups={{0,2,4,6},{8,10,12,14},{16,18,20,22},{24,26,28,30},{1,3,5,7},{9,11,13,1..., dimensions={0}, use_global_device_ids=true | all-gather | bytes 2560 | tf_op jit(solution)/shard_map/all_gather | solution.py:65
  125.5 11.2 %all-gather.4 = f32[4,1,128]{2,1,0:T(1,128)S(1)} all-gather(f32[1,1,128]{2,1,0:T(1,128)S(1)} %bitcast.13), channel_id=4, replica_groups={{0,8,16,24},{2,10,18,26},{4,12,20,28},{6,14,22,30},{1,9,17,25},{3,11,19..., dimensions={0}, use_global_device_ids=true | all-gather | bytes 2560 | tf_op jit(solution)/shard_map/all_gather | solution.py:65
  136.6 0.6 reduce.5
  (4 shorter events, 0.1 us)
Async XLA Ops:
  7.2 88.5 %all-gather.7.cloned.1.call-start = ((), (), s32[]{:S(2)}) async-start(), calls=%async_computation.2 | async-start | bytes 8650752 | tf_op jit(solution)/shard_map/all_gather | solution.py:54
Sparse Core Ops, SparseCore 0:
  10.7 84.8 all-gather.6

commit v4 on v3

--- a/solution.py
+++ b/solution.py
@@ -1,3 +1,5 @@
+import functools
+
 import jax
 import jax.numpy as jnp
 from jax import lax
@@ -39,9 +41,75 @@
     )(layer[None], mask, matrix)
 
 
-def total_over(value, axis, size):
-    copies = jnp.broadcast_to(value, (size,) + value.shape)
-    return jnp.sum(lax.all_to_all(copies, axis, 0, 0, tiled=True), 0)
+def product_kernel(ahead, a_ref, b_ref, out_ref, squares_ref, a_held, b_held, a_came, b_came):
+    count = a_ref.shape[0]
+
+    def copies(n):
+        return (
+            pltpu.make_async_copy(b_ref.at[n], b_held.at[n], b_came.at[n]),
+            pltpu.make_async_copy(a_ref.at[n], a_held.at[n], a_came.at[n]),
+        )
+
+    for n in range(min(ahead, count)):
+        for copy in copies(n):
+            copy.start()
+    total = None
+    for n in range(count):
+        for copy in copies(n):
+            copy.wait()
+        if n + ahead < count:
+            for copy in copies(n + ahead):
+                copy.start()
+        part = jnp.dot(a_held[n], b_held[n], preferred_element_type=jnp.float32)
+        total = part if total is None else total + part
+    out_ref[...] = total.astype(out_ref.dtype)
+    squares = jnp.sum(jnp.square(total).reshape(-1, 8, total.shape[1]), 0)
+    squares_ref[...] = jnp.sum(squares[:, :128] + squares[:, 128:], 0, keepdims=True)
+
+
+def multiply(a_all, b_all):
+    count, rows, depth = a_all.shape
+    cols = b_all.shape[2]
+    vmem = pl.BlockSpec(memory_space=pltpu.VMEM)
+    hbm = pl.BlockSpec(memory_space=pl.ANY)
+    return pl.pallas_call(
+        functools.partial(product_kernel, 8),
+        in_specs=[hbm, hbm],
+        out_specs=[vmem, vmem],
+        out_shape=[
+            jax.ShapeDtypeStruct((rows, cols), a_all.dtype),
+            jax.ShapeDtypeStruct((1, 128), jnp.float32),
+        ],
+        scratch_shapes=[
+            pltpu.VMEM(a_all.shape, a_all.dtype),
+            pltpu.VMEM(b_all.shape, b_all.dtype),
+            pltpu.SemaphoreType.DMA((count,)),
+            pltpu.SemaphoreType.DMA((count,)),
+        ],
+        compiler_params=pltpu.CompilerParams(vmem_limit_bytes=57 << 20),
+        cost_estimate=pl.CostEstimate(
+            flops=2 * count * rows * depth * cols,
+            bytes_accessed=2 * (a_all.size + b_all.size),
+            transcendentals=0,
+        ),
+    )(a_all, b_all)
+
+
+def total_over_all(value, count, layers, near=4):
+    far = count // near
+    runs = [
+        [(r * count + run * near + c) * layers + d
+         for r in range(count) for c in range(near) for d in range(layers)]
+        for run in range(far)
+    ]
+    copies = jnp.broadcast_to(value, (len(runs[0]),) + value.shape)
+    value = jnp.sum(
+        lax.all_to_all(
+            copies, ("row", "col", "depth"), 0, 0, tiled=True, axis_index_groups=runs
+        ), 0
+    )
+    apart = [[run * near + c for run in range(far)] for c in range(near)]
+    return jnp.sum(lax.all_gather(value, "col", axis_index_groups=apart), (0, 1, 2))
 
 
 def per_device(a_matrix, b_matrix, mask_a, mask_b):
@@ -49,23 +117,16 @@
     layers = lax.axis_size("depth")
     count = lax.axis_size("row")
     width = a_matrix.shape[0]
-    share = width // layers
     a_part = masked_half(layer, mask_a, a_matrix)
     a_all = lax.all_gather(a_part, ("col", "depth"), axis=0)
     b_part = masked_half(layer, mask_b, b_matrix)
     copies = jnp.broadcast_to(b_part, (count,) + b_part.shape)
     b_all = lax.all_to_all(copies, "row", 0, 0, tiled=True)
-    b_all = b_all.reshape(count * layers, share, share)
-    full = jnp.einsum("smk,skn->mn", a_all, b_all, preferred_element_type=jnp.float32)
-    squares = jnp.sum(jnp.square(full).reshape(-1, 1, 128), 0)
-    squares = total_over(squares, ("row", "depth"), count * layers)
-    near = [[4 * g + i for i in range(4)] for g in range(count // 4)]
-    far = [[4 * g + i for g in range(count // 4)] for i in range(4)]
-    for groups in (near, far):
-        squares = jnp.sum(lax.all_gather(squares, "col", axis_index_groups=groups), 0)
+    product, squares = multiply(a_all, b_all.reshape(a_all.shape[0], -1, b_all.shape[2]))
+    squares = total_over_all(squares, count, layers)
     entries = float(width * count * (width * count))
-    rms_norm = jnp.sqrt(jnp.sum(squares) / entries + 1e-06)
-    return (full.astype(jnp.bfloat16), rms_norm)
+    rms_norm = jnp.sqrt(squares / entries + 1e-06)
+    return (product, rms_norm)
 
 
 def solution(mesh):

time: 148 us -> 146 us (0.986)
  Pallas kernels: 3.65 us -> 11.7 us
  matrix products: 7.6 us -> 0 us
  blocking collectives: 89.1 us -> 87.1 us
    pallas_call x0 -> x1, Pallas kernels: none -> 8.03 us  [multiply(): pl.pallas_call(functools.partial(product_kernel, 8), in_specs=[hbm, hbm],...]
    all_gather x2 -> x1, blocking collectives: 19.1 us -> 11.2 us  [total_over_all(): lax.all_gather(value, 'col', axis_index_groups=apart)]
    dot_general x1 -> x0, matrix products: 7.6 us -> none  [per_device(): jnp.einsum('smk,skn->mn', a_all, b_all, preferred_element_type=jnp.float32)]
    all_to_all x1, blocking collectives: 14 us -> 19.9 us  [total_over_all(): lax.all_to_all(copies, ('row', 'col', 'depth'), 0, 0, tiled=True, axis_in...]
where the time goes in v4:
time: 146 us; the launch traced here: 145 us
  blocking collectives  87.1 us (60%)
  waiting for transfers between devices  27.4 us (19%)
  between operations  15.9 us (11%)
  Pallas kernels  11.7 us (8%)
  local copies, waits for them, and re-layouts  2.04 us (1%)
    all_to_all x1, blocking collectives, per_device(): b_all = lax.all_to_all(copies, 'row', 0, 0, tiled=True)  56 us
    all_gather x1, waiting for transfers between devices, per_device(): a_all = lax.all_gather(a_part, ('col', 'depth'), axis=0)  27.4 us
    all_to_all x1, blocking collectives, total_over_all(): lax.all_to_all(copies, ('row', 'col', 'depth'), 0, 0, tiled=True, axis_in...  19.9 us
    all_gather x1, blocking collectives, total_over_all(): lax.all_gather(value, 'col', axis_index_groups=apart)  11.2 us
    pallas_call x1, Pallas kernels, multiply(): pl.pallas_call(functools.partial(product_kernel, 8), in_specs=[hbm, hbm],...  8.03 us
    pallas_call x2, Pallas kernels, masked_half(): pl.pallas_call(mask_kernel, in_specs=[smem, smem, vmem], out_specs=vmem,...  3.65 us
  transfers between devices with their start and end apart: 1, of which 1 were waited for; matrix products, arithmetic and copies ran while one was open for 1% of the time, Pallas kernels for 1%

profile of v4, /device:TPU:1, one launch (start us, length us, event | category | flops | bytes accessed | tf_op | source)
XLA Modules:
  0.0 144.8 jit_solution(3255920858871856464)
XLA Ops:
  7.2 0.0 all-gather.5.cloned.1.call-start
  7.2 1.8 %shard_map.59 = bf16[512,256]{1,0:T(8,128)(2,1)} custom-call(s32[1]{0:T(128)} %bitcast.layer_ref, s32[4,4]{1,0:T(4,128)} %mask_ref.2, bf16[512,512]{1,0:T(8,128)(2,1)} %matrix_ref.2), custom_call_target="tpu_custom_call" | custom-call | bytes 786432 | tf_op jit(solution)/shard_map/pallas_call | solution.py:32
  9.0 0.0 all-gather.5.cloned.1.call-update
  9.1 1.8 %shard_map.60 = bf16[512,256]{1,0:T(8,128)(2,1)} custom-call(s32[1]{0:T(128)} %bitcast.layer_ref, s32[4,4]{1,0:T(4,128)} %mask_ref.3, bf16[512,512]{1,0:T(8,128)(2,1)} %matrix_ref.3), custom_call_target="tpu_custom_call" | custom-call | bytes 786432 | tf_op jit(solution)/shard_map/pallas_call | solution.py:32
  10.9 1.3 broadcast_in_dim.11
  12.2 56.0 %all_to_all.10 = bf16[16,512,256]{2,1,0:T(8,128)(2,1)} all-to-all(bf16[16,512,256]{2,1,0:T(8,128)(2,1)S(1)} %broadcast_in_dim.11), channel_id=1, replica_groups=mesh['row'=16,'col'=16,'depth'=2] {'row'}, dimensions={0} | all-to-all | bytes 8388608 | tf_op jit(solution)/shard_map/all_to_all | solution.py:124
  68.2 27.4 %all-gather.5.cloned.1.call-done = bf16[16384,256]{1,0:T(8,128)(2,1)} async-done(((bf16[512,256]{1,0:T(8,128)(2,1)}), bf16[16384,256]{1,0:T(8,128)(2,1)}) %all-gather.5.cloned.1.call-update) | async-done | bytes 8388624 | tf_op jit(solution)/shard_map/all_gather | solution.py:121
  95.6 8.0 %shard_map.61 = (bf16[512,256]{1,0:T(8,128)(2,1)}, f32[1,128]{1,0:T(1,128)}) custom-call(bf16[32,512,256]{2,1,0:T(8,128)(2,1)} %bitcast.7, bf16[32,256,256]{2,1,0:T(8,128)(2,1)} %bitcast.6), custom_call_target="tpu_custom_call" | custom-call | flops 2147483648 | bytes 12582912 | tf_op jit(solution)/shard_map/pallas_call | solution.py:75
  103.7 0.7 broadcast_in_dim.12
  104.4 19.9 %all_to_all.11 = f32[128,1,128]{2,1,0:T(1,128)S(1)} all-to-all(f32[128,1,128]{2,1,0:T(1,128)S(1)} %broadcast_in_dim.12), channel_id=1, replica_groups={{0,1,2,3,4,5,6,7,32,33,34,35,36,37,38,39,64,65,66,67,68,69,70,71,96,97,..., dimensions={0} | all-to-all | bytes 131072 | tf_op jit(solution)/shard_map/all_to_all | solution.py:107
  124.3 11.2 %all-gather.2 = f32[4,1,128]{2,1,0:T(1,128)S(1)} all-gather(f32[1,1,128]{2,1,0:T(1,128)S(1)} %bitcast.9), channel_id=3, replica_groups={{0,8,16,24},{2,10,18,26},{4,12,20,28},{6,14,22,30},{1,9,17,25},{3,11,19..., dimensions={0}, use_global_device_ids=true | all-gather | bytes 2560 | tf_op jit(solution)/shard_map/all_gather | solution.py:112
  135.5 0.6 reduce.1
  (1 shorter events, 0.0 us)
Async XLA Ops:
  7.2 88.5 %all-gather.5.cloned.1.call-start = ((), (), s32[]{:S(2)}) async-start(), calls=%async_computation.2 | async-start | bytes 8650752 | tf_op jit(solution)/shard_map/all_gather | solution.py:121
Sparse Core Ops, SparseCore 0:
  10.7 84.8 all-gather.4

commit v5 on v4

--- a/solution.py
+++ b/solution.py
@@ -42,7 +42,7 @@
 
 
 def product_kernel(ahead, a_ref, b_ref, out_ref, squares_ref, a_held, b_held, a_came, b_came):
-    count = a_ref.shape[0]
+    count, rows = a_ref.shape[0], a_ref.shape[1] // 2
 
     def copies(n):
         return (
@@ -53,32 +53,39 @@
     for n in range(min(ahead, count)):
         for copy in copies(n):
             copy.start()
-    total = None
+    totals = [None, None]
     for n in range(count):
         for copy in copies(n):
             copy.wait()
         if n + ahead < count:
             for copy in copies(n + ahead):
                 copy.start()
-        part = jnp.dot(a_held[n], b_held[n], preferred_element_type=jnp.float32)
-        total = part if total is None else total + part
-    out_ref[...] = total.astype(out_ref.dtype)
-    squares = jnp.sum(jnp.square(total).reshape(-1, 8, total.shape[1]), 0)
-    squares_ref[...] = jnp.sum(squares[:, :128] + squares[:, 128:], 0, keepdims=True)
+        for h in range(2):
+            part = jnp.dot(
+                a_held[n, h * rows:(h + 1) * rows], b_held[n],
+                preferred_element_type=jnp.float32,
+            )
+            totals[h] = part if totals[h] is None else totals[h] + part
+    squares = None
+    for h, total in enumerate(totals):
+        out_ref[h * rows:(h + 1) * rows] = total.astype(out_ref.dtype)
+        more = jnp.sum(jnp.square(total).reshape(-1, 8, total.shape[1]), 0)
+        squares = more if squares is None else squares + more
+    squares = jnp.sum(squares[:, :128] + squares[:, 128:], 0, keepdims=True)
+    squares_ref[...] = jnp.broadcast_to(squares[None], squares_ref.shape)
 
 
-def multiply(a_all, b_all):
+def multiply(a_all, b_all, copies):
     count, rows, depth = a_all.shape
     cols = b_all.shape[2]
     vmem = pl.BlockSpec(memory_space=pltpu.VMEM)
-    hbm = pl.BlockSpec(memory_space=pl.ANY)
     return pl.pallas_call(
-        functools.partial(product_kernel, 8),
-        in_specs=[hbm, hbm],
+        functools.partial(product_kernel, 12),
+        in_specs=[pl.BlockSpec(memory_space=pl.ANY)] * 2,
         out_specs=[vmem, vmem],
         out_shape=[
             jax.ShapeDtypeStruct((rows, cols), a_all.dtype),
-            jax.ShapeDtypeStruct((1, 128), jnp.float32),
+            jax.ShapeDtypeStruct((copies, 1, 128), jnp.float32),
         ],
         scratch_shapes=[
             pltpu.VMEM(a_all.shape, a_all.dtype),
@@ -95,20 +102,21 @@
     )(a_all, b_all)
 
 
-def total_over_all(value, count, layers, near=4):
-    far = count // near
-    runs = [
+def near_runs(count, layers, near):
+    return [
         [(r * count + run * near + c) * layers + d
          for r in range(count) for c in range(near) for d in range(layers)]
-        for run in range(far)
+        for run in range(count // near)
     ]
-    copies = jnp.broadcast_to(value, (len(runs[0]),) + value.shape)
+
+
+def total_over_all(copies, count, runs, near):
     value = jnp.sum(
         lax.all_to_all(
             copies, ("row", "col", "depth"), 0, 0, tiled=True, axis_index_groups=runs
         ), 0
     )
-    apart = [[run * near + c for run in range(far)] for c in range(near)]
+    apart = [[run * near + c for run in range(len(runs))] for c in range(near)]
     return jnp.sum(lax.all_gather(value, "col", axis_index_groups=apart), (0, 1, 2))
 
 
@@ -122,8 +130,11 @@
     b_part = masked_half(layer, mask_b, b_matrix)
     copies = jnp.broadcast_to(b_part, (count,) + b_part.shape)
     b_all = lax.all_to_all(copies, "row", 0, 0, tiled=True)
-    product, squares = multiply(a_all, b_all.reshape(a_all.shape[0], -1, b_all.shape[2]))
-    squares = total_over_all(squares, count, layers)
+    b_all = b_all.reshape(a_all.shape[0], -1, b_all.shape[2])
+    near = 4
+    runs = near_runs(count, layers, near)
+    product, copies = multiply(a_all, b_all, len(runs[0]))
+    squares = total_over_all(copies, count, runs, near)
     entries = float(width * count * (width * count))
     rms_norm = jnp.sqrt(squares / entries + 1e-06)
     return (product, rms_norm)

time: 146 us -> 144 us (0.986)
  Pallas kernels: 11.7 us -> 10 us
    pallas_call x1, Pallas kernels: 8.03 us -> 6.38 us  [multiply(): pl.pallas_call(functools.partial(product_kernel, 12), in_specs=[pl.BlockS...]
where the time goes in v5:
time: 144 us; the launch traced here: 143 us
  blocking collectives  87.3 us (61%)
  waiting for transfers between devices  27.4 us (19%)
  between operations  15.9 us (11%)
  Pallas kernels  10 us (7%)
    all_to_all x1, blocking collectives, per_device(): b_all = lax.all_to_all(copies, 'row', 0, 0, tiled=True)  56 us
    all_gather x1, waiting for transfers between devices, per_device(): a_all = lax.all_gather(a_part, ('col', 'depth'), axis=0)  27.4 us
    all_to_all x1, blocking collectives, total_over_all(): lax.all_to_all(copies, ('row', 'col', 'depth'), 0, 0, tiled=True, axis_in...  20.1 us
    all_gather x1, blocking collectives, total_over_all(): lax.all_gather(value, 'col', axis_index_groups=apart)  11.2 us
    pallas_call x1, Pallas kernels, multiply(): pl.pallas_call(functools.partial(product_kernel, 12), in_specs=[pl.BlockS...  6.38 us
    pallas_call x2, Pallas kernels, masked_half(): pl.pallas_call(mask_kernel, in_specs=[smem, smem, vmem], out_specs=vmem,...  3.65 us
  transfers between devices with their start and end apart: 1, of which 1 were waited for; matrix products, arithmetic and copies ran while one was open for 1% of the time, Pallas kernels for 1%

profile of v5, /device:TPU:1, one launch (start us, length us, event | category | flops | bytes accessed | tf_op | source)
XLA Modules:
  0.0 142.8 jit_solution(14672627126237792156)
XLA Ops:
  7.2 0.0 all-gather.5.cloned.1.call-start
  7.2 1.8 %shard_map.59 = bf16[512,256]{1,0:T(8,128)(2,1)} custom-call(s32[1]{0:T(128)} %bitcast.layer_ref, s32[4,4]{1,0:T(4,128)} %mask_ref.2, bf16[512,512]{1,0:T(8,128)(2,1)} %matrix_ref.2), custom_call_target="tpu_custom_call" | custom-call | bytes 786432 | tf_op jit(solution)/shard_map/pallas_call | solution.py:32
  9.0 0.0 all-gather.5.cloned.1.call-update
  9.1 1.8 %shard_map.60 = bf16[512,256]{1,0:T(8,128)(2,1)} custom-call(s32[1]{0:T(128)} %bitcast.layer_ref, s32[4,4]{1,0:T(4,128)} %mask_ref.3, bf16[512,512]{1,0:T(8,128)(2,1)} %matrix_ref.3), custom_call_target="tpu_custom_call" | custom-call | bytes 786432 | tf_op jit(solution)/shard_map/pallas_call | solution.py:32
  10.9 1.3 broadcast_in_dim.8
  12.2 56.0 %all_to_all.10 = bf16[16,512,256]{2,1,0:T(8,128)(2,1)} all-to-all(bf16[16,512,256]{2,1,0:T(8,128)(2,1)S(1)} %broadcast_in_dim.8), channel_id=1, replica_groups=mesh['row'=16,'col'=16,'depth'=2] {'row'}, dimensions={0} | all-to-all | bytes 8388608 | tf_op jit(solution)/shard_map/all_to_all | solution.py:132
  68.2 27.4 %all-gather.5.cloned.1.call-done = bf16[16384,256]{1,0:T(8,128)(2,1)} async-done(((bf16[512,256]{1,0:T(8,128)(2,1)}), bf16[16384,256]{1,0:T(8,128)(2,1)}) %all-gather.5.cloned.1.call-update) | async-done | bytes 8388624 | tf_op jit(solution)/shard_map/all_gather | solution.py:129
  95.6 6.4 %shard_map.61 = (bf16[512,256]{1,0:T(8,128)(2,1)}, f32[128,1,128]{2,1,0:T(1,128)}) custom-call(bf16[32,512,256]{2,1,0:T(8,128)(2,1)} %bitcast.5, bf16[32,256,256]{2,1,0:T(8,128)(2,1)} %bitcast.4), custom_call_target="tpu_custom_call" | custom-call | flops 2147483648 | bytes 12582912 | tf_op jit(solution)/shard_map/pallas_call | solution.py:82
  102.0 20.1 %all_to_all.11 = f32[128,1,128]{2,1,0:T(1,128)S(1)} all-to-all(f32[128,1,128]{2,1,0:T(1,128)} %get-tuple-element.5), channel_id=1, replica_groups={{0,1,2,3,4,5,6,7,32,33,34,35,36,37,38,39,64,65,66,67,68,69,70,71,96,97,..., dimensions={0} | all-to-all | bytes 131072 | tf_op jit(solution)/shard_map/all_to_all | solution.py:115
  122.2 0.2 reduce_sum.18
  122.3 11.2 %all-gather.2 = f32[4,1,128]{2,1,0:T(1,128)S(1)} all-gather(f32[1,1,128]{2,1,0:T(1,128)S(1)} %bitcast.6), channel_id=3, replica_groups={{0,8,16,24},{2,10,18,26},{4,12,20,28},{6,14,22,30},{1,9,17,25},{3,11,19..., dimensions={0}, use_global_device_ids=true | all-gather | bytes 2560 | tf_op jit(solution)/shard_map/all_gather | solution.py:120
  133.5 0.6 reduce.1
Async XLA Ops:
  7.2 88.5 %all-gather.5.cloned.1.call-start = ((), (), s32[]{:S(2)}) async-start(), calls=%async_computation.2 | async-start | bytes 8650752 | tf_op jit(solution)/shard_map/all_gather | solution.py:129
Sparse Core Ops, SparseCore 0:
  10.7 84.8 all-gather.4

commit v6 on v5

--- a/solution.py
+++ b/solution.py
@@ -41,25 +41,24 @@
     )(layer[None], mask, matrix)
 
 
-def product_kernel(ahead, a_ref, b_ref, out_ref, squares_ref, a_held, b_held, a_came, b_came):
+def product_kernel(group, a_ref, b_ref, out_ref, squares_ref, a_held, b_held, a_came, b_came):
     count, rows = a_ref.shape[0], a_ref.shape[1] // 2
 
-    def copies(n):
+    def copies(first):
+        some = pl.ds(first, group)
         return (
-            pltpu.make_async_copy(b_ref.at[n], b_held.at[n], b_came.at[n]),
-            pltpu.make_async_copy(a_ref.at[n], a_held.at[n], a_came.at[n]),
+            pltpu.make_async_copy(b_ref.at[some], b_held.at[some], b_came.at[first // group]),
+            pltpu.make_async_copy(a_ref.at[some], a_held.at[some], a_came.at[first // group]),
         )
 
-    for n in range(min(ahead, count)):
-        for copy in copies(n):
+    for first in range(0, count, group):
+        for copy in copies(first):
             copy.start()
     totals = [None, None]
     for n in range(count):
-        for copy in copies(n):
-            copy.wait()
-        if n + ahead < count:
-            for copy in copies(n + ahead):
-                copy.start()
+        if n % group == 0:
+            for copy in copies(n):
+                copy.wait()
         for h in range(2):
             part = jnp.dot(
                 a_held[n, h * rows:(h + 1) * rows], b_held[n],
@@ -80,7 +79,7 @@
     cols = b_all.shape[2]
     vmem = pl.BlockSpec(memory_space=pltpu.VMEM)
     return pl.pallas_call(
-        functools.partial(product_kernel, 12),
+        functools.partial(product_kernel, 2),
         in_specs=[pl.BlockSpec(memory_space=pl.ANY)] * 2,
         out_specs=[vmem, vmem],
         out_shape=[

time: 144 us -> 144 us (level)
  no operation moved by 1% of the time
where the time goes in v6:
time: 144 us; the launch traced here: 143 us
  blocking collectives  87.3 us (61%)
  waiting for transfers between devices  27.4 us (19%)
  between operations  15.9 us (11%)
  Pallas kernels  9.79 us (7%)
    all_to_all x1, blocking collectives, per_device(): b_all = lax.all_to_all(copies, 'row', 0, 0, tiled=True)  56 us
    all_gather x1, waiting for transfers between devices, per_device(): a_all = lax.all_gather(a_part, ('col', 'depth'), axis=0)  27.4 us
    all_to_all x1, blocking collectives, total_over_all(): lax.all_to_all(copies, ('row', 'col', 'depth'), 0, 0, tiled=True, axis_in...  20.1 us
    all_gather x1, blocking collectives, total_over_all(): lax.all_gather(value, 'col', axis_index_groups=apart)  11.2 us
    pallas_call x1, Pallas kernels, multiply(): pl.pallas_call(functools.partial(product_kernel, 2), in_specs=[pl.BlockSp...  6.14 us
    pallas_call x2, Pallas kernels, masked_half(): pl.pallas_call(mask_kernel, in_specs=[smem, smem, vmem], out_specs=vmem,...  3.65 us
  transfers between devices with their start and end apart: 1, of which 1 were waited for; matrix products, arithmetic and copies ran while one was open for 1% of the time, Pallas kernels for 1%

profile of v6, /device:TPU:1, one launch (start us, length us, event | category | flops | bytes accessed | tf_op | source)
XLA Modules:
  0.0 142.5 jit_solution(10402642998479247238)
XLA Ops:
  7.2 0.0 all-gather.5.cloned.1.call-start
  7.2 1.8 %shard_map.59 = bf16[512,256]{1,0:T(8,128)(2,1)} custom-call(s32[1]{0:T(128)} %bitcast.layer_ref, s32[4,4]{1,0:T(4,128)} %mask_ref.2, bf16[512,512]{1,0:T(8,128)(2,1)} %matrix_ref.2), custom_call_target="tpu_custom_call" | custom-call | bytes 786432 | tf_op jit(solution)/shard_map/pallas_call | solution.py:32
  9.0 0.0 all-gather.5.cloned.1.call-update
  9.1 1.8 %shard_map.60 = bf16[512,256]{1,0:T(8,128)(2,1)} custom-call(s32[1]{0:T(128)} %bitcast.layer_ref, s32[4,4]{1,0:T(4,128)} %mask_ref.3, bf16[512,512]{1,0:T(8,128)(2,1)} %matrix_ref.3), custom_call_target="tpu_custom_call" | custom-call | bytes 786432 | tf_op jit(solution)/shard_map/pallas_call | solution.py:32
  10.9 1.3 broadcast_in_dim.8
  12.2 56.0 %all_to_all.10 = bf16[16,512,256]{2,1,0:T(8,128)(2,1)} all-to-all(bf16[16,512,256]{2,1,0:T(8,128)(2,1)S(1)} %broadcast_in_dim.8), channel_id=1, replica_groups=mesh['row'=16,'col'=16,'depth'=2] {'row'}, dimensions={0} | all-to-all | bytes 8388608 | tf_op jit(solution)/shard_map/all_to_all | solution.py:131
  68.2 27.4 %all-gather.5.cloned.1.call-done = bf16[16384,256]{1,0:T(8,128)(2,1)} async-done(((bf16[512,256]{1,0:T(8,128)(2,1)}), bf16[16384,256]{1,0:T(8,128)(2,1)}) %all-gather.5.cloned.1.call-update) | async-done | bytes 8388624 | tf_op jit(solution)/shard_map/all_gather | solution.py:128
  95.6 6.1 %shard_map.61 = (bf16[512,256]{1,0:T(8,128)(2,1)}, f32[128,1,128]{2,1,0:T(1,128)}) custom-call(bf16[32,512,256]{2,1,0:T(8,128)(2,1)} %bitcast.5, bf16[32,256,256]{2,1,0:T(8,128)(2,1)} %bitcast.4), custom_call_target="tpu_custom_call" | custom-call | flops 2147483648 | bytes 12582912 | tf_op jit(solution)/shard_map/pallas_call | solution.py:81
  101.8 20.1 %all_to_all.11 = f32[128,1,128]{2,1,0:T(1,128)S(1)} all-to-all(f32[128,1,128]{2,1,0:T(1,128)} %get-tuple-element.5), channel_id=1, replica_groups={{0,1,2,3,4,5,6,7,32,33,34,35,36,37,38,39,64,65,66,67,68,69,70,71,96,97,..., dimensions={0} | all-to-all | bytes 131072 | tf_op jit(solution)/shard_map/all_to_all | solution.py:114
  121.9 0.2 reduce_sum.18
  122.1 11.2 %all-gather.2 = f32[4,1,128]{2,1,0:T(1,128)S(1)} all-gather(f32[1,1,128]{2,1,0:T(1,128)S(1)} %bitcast.6), channel_id=3, replica_groups={{0,8,16,24},{2,10,18,26},{4,12,20,28},{6,14,22,30},{1,9,17,25},{3,11,19..., dimensions={0}, use_global_device_ids=true | all-gather | bytes 2560 | tf_op jit(solution)/shard_map/all_gather | solution.py:119
  133.2 0.6 reduce.1
Async XLA Ops:
  7.2 88.5 %all-gather.5.cloned.1.call-start = ((), (), s32[]{:S(2)}) async-start(), calls=%async_computation.2 | async-start | bytes 8650752 | tf_op jit(solution)/shard_map/all_gather | solution.py:128
Sparse Core Ops, SparseCore 0:
  10.7 84.8 all-gather.4

commit v7 on v6

--- a/solution.py
+++ b/solution.py
@@ -44,19 +44,23 @@
 def product_kernel(group, a_ref, b_ref, out_ref, squares_ref, a_held, b_held, a_came, b_came):
     count, rows = a_ref.shape[0], a_ref.shape[1] // 2
 
+    sizes = [1, 1] + [group] * ((count - 2) // group)
+    firsts = {sum(sizes[:m]): m for m in range(len(sizes))}
+
     def copies(first):
-        some = pl.ds(first, group)
+        m = firsts[first]
+        some = pl.ds(first, sizes[m])
         return (
-            pltpu.make_async_copy(b_ref.at[some], b_held.at[some], b_came.at[first // group]),
-            pltpu.make_async_copy(a_ref.at[some], a_held.at[some], a_came.at[first // group]),
+            pltpu.make_async_copy(b_ref.at[some], b_held.at[some], b_came.at[m]),
+            pltpu.make_async_copy(a_ref.at[some], a_held.at[some], a_came.at[m]),
         )
 
-    for first in range(0, count, group):
+    for first in firsts:
         for copy in copies(first):
             copy.start()
     totals = [None, None]
     for n in range(count):
-        if n % group == 0:
+        if n in firsts:
             for copy in copies(n):
                 copy.wait()
         for h in range(2):

time: 144 us -> 144 us (level)
  no operation moved by 1% of the time
where the time goes in v7:
time: 144 us; the launch traced here: 143 us
  blocking collectives  87.3 us (61%)
  waiting for transfers between devices  27.4 us (19%)
  between operations  15.9 us (11%)
  Pallas kernels  9.84 us (7%)
    all_to_all x1, blocking collectives, per_device(): b_all = lax.all_to_all(copies, 'row', 0, 0, tiled=True)  56 us
    all_gather x1, waiting for transfers between devices, per_device(): a_all = lax.all_gather(a_part, ('col', 'depth'), axis=0)  27.4 us
    all_to_all x1, blocking collectives, total_over_all(): lax.all_to_all(copies, ('row', 'col', 'depth'), 0, 0, tiled=True, axis_in...  20.1 us
    all_gather x1, blocking collectives, total_over_all(): lax.all_gather(value, 'col', axis_index_groups=apart)  11.2 us
    pallas_call x1, Pallas kernels, multiply(): pl.pallas_call(functools.partial(product_kernel, 2), in_specs=[pl.BlockSp...  6.19 us
    pallas_call x2, Pallas kernels, masked_half(): pl.pallas_call(mask_kernel, in_specs=[smem, smem, vmem], out_specs=vmem,...  3.65 us
  transfers between devices with their start and end apart: 1, of which 1 were waited for; matrix products, arithmetic and copies ran while one was open for 1% of the time, Pallas kernels for 1%

profile of v7, /device:TPU:1, one launch (start us, length us, event | category | flops | bytes accessed | tf_op | source)
XLA Modules:
  0.0 142.6 jit_solution(7762775892001959482)
XLA Ops:
  7.2 0.0 all-gather.5.cloned.1.call-start
  7.2 1.8 %shard_map.59 = bf16[512,256]{1,0:T(8,128)(2,1)} custom-call(s32[1]{0:T(128)} %bitcast.layer_ref, s32[4,4]{1,0:T(4,128)} %mask_ref.2, bf16[512,512]{1,0:T(8,128)(2,1)} %matrix_ref.2), custom_call_target="tpu_custom_call" | custom-call | bytes 786432 | tf_op jit(solution)/shard_map/pallas_call | solution.py:32
  9.0 0.0 all-gather.5.cloned.1.call-update
  9.1 1.8 %shard_map.60 = bf16[512,256]{1,0:T(8,128)(2,1)} custom-call(s32[1]{0:T(128)} %bitcast.layer_ref, s32[4,4]{1,0:T(4,128)} %mask_ref.3, bf16[512,512]{1,0:T(8,128)(2,1)} %matrix_ref.3), custom_call_target="tpu_custom_call" | custom-call | bytes 786432 | tf_op jit(solution)/shard_map/pallas_call | solution.py:32
  10.9 1.3 broadcast_in_dim.8
  12.2 56.0 %all_to_all.10 = bf16[16,512,256]{2,1,0:T(8,128)(2,1)} all-to-all(bf16[16,512,256]{2,1,0:T(8,128)(2,1)S(1)} %broadcast_in_dim.8), channel_id=1, replica_groups=mesh['row'=16,'col'=16,'depth'=2] {'row'}, dimensions={0} | all-to-all | bytes 8388608 | tf_op jit(solution)/shard_map/all_to_all | solution.py:135
  68.2 27.4 %all-gather.5.cloned.1.call-done = bf16[16384,256]{1,0:T(8,128)(2,1)} async-done(((bf16[512,256]{1,0:T(8,128)(2,1)}), bf16[16384,256]{1,0:T(8,128)(2,1)}) %all-gather.5.cloned.1.call-update) | async-done | bytes 8388624 | tf_op jit(solution)/shard_map/all_gather | solution.py:132
  95.6 6.2 %shard_map.61 = (bf16[512,256]{1,0:T(8,128)(2,1)}, f32[128,1,128]{2,1,0:T(1,128)}) custom-call(bf16[32,512,256]{2,1,0:T(8,128)(2,1)} %bitcast.5, bf16[32,256,256]{2,1,0:T(8,128)(2,1)} %bitcast.4), custom_call_target="tpu_custom_call" | custom-call | flops 2147483648 | bytes 12582912 | tf_op jit(solution)/shard_map/pallas_call | solution.py:85
  101.8 20.1 %all_to_all.11 = f32[128,1,128]{2,1,0:T(1,128)S(1)} all-to-all(f32[128,1,128]{2,1,0:T(1,128)} %get-tuple-element.5), channel_id=1, replica_groups={{0,1,2,3,4,5,6,7,32,33,34,35,36,37,38,39,64,65,66,67,68,69,70,71,96,97,..., dimensions={0} | all-to-all | bytes 131072 | tf_op jit(solution)/shard_map/all_to_all | solution.py:118
  122.0 0.2 reduce_sum.18
  122.1 11.2 %all-gather.2 = f32[4,1,128]{2,1,0:T(1,128)S(1)} all-gather(f32[1,1,128]{2,1,0:T(1,128)S(1)} %bitcast.6), channel_id=3, replica_groups={{0,8,16,24},{2,10,18,26},{4,12,20,28},{6,14,22,30},{1,9,17,25},{3,11,19..., dimensions={0}, use_global_device_ids=true | all-gather | bytes 2560 | tf_op jit(solution)/shard_map/all_gather | solution.py:123
  133.3 0.6 reduce.1
Async XLA Ops:
  7.2 88.5 %all-gather.5.cloned.1.call-start = ((), (), s32[]{:S(2)}) async-start(), calls=%async_computation.2 | async-start | bytes 8650752 | tf_op jit(solution)/shard_map/all_gather | solution.py:132
Sparse Core Ops, SparseCore 0:
  10.7 84.8 all-gather.4

commit v8 on v6

--- a/solution.py
+++ b/solution.py
@@ -130,7 +130,7 @@
     copies = jnp.broadcast_to(b_part, (count,) + b_part.shape)
     b_all = lax.all_to_all(copies, "row", 0, 0, tiled=True)
     b_all = b_all.reshape(a_all.shape[0], -1, b_all.shape[2])
-    near = 4
+    near = 2
     runs = near_runs(count, layers, near)
     product, copies = multiply(a_all, b_all, len(runs[0]))
     squares = total_over_all(copies, count, runs, near)

time: 144 us -> 144 us (level)
    all_to_all x1, blocking collectives: 20.1 us -> 16.5 us  [total_over_all(): lax.all_to_all(copies, ('row', 'col', 'depth'), 0, 0, tiled=True, axis_in...]
    all_gather x1, blocking collectives: 11.2 us -> 13.9 us  [total_over_all(): lax.all_gather(value, 'col', axis_index_groups=apart)]
where the time goes in v8:
time: 144 us; the launch traced here: 142 us
  blocking collectives  86.3 us (60%)
  waiting for transfers between devices  27.4 us (19%)
  between operations  15.9 us (11%)
  Pallas kernels  9.79 us (7%)
    all_to_all x1, blocking collectives, per_device(): b_all = lax.all_to_all(copies, 'row', 0, 0, tiled=True)  56 us
    all_gather x1, waiting for transfers between devices, per_device(): a_all = lax.all_gather(a_part, ('col', 'depth'), axis=0)  27.4 us
    all_to_all x1, blocking collectives, total_over_all(): lax.all_to_all(copies, ('row', 'col', 'depth'), 0, 0, tiled=True, axis_in...  16.5 us
    all_gather x1, blocking collectives, total_over_all(): lax.all_gather(value, 'col', axis_index_groups=apart)  13.9 us
    pallas_call x1, Pallas kernels, multiply(): pl.pallas_call(functools.partial(product_kernel, 2), in_specs=[pl.BlockSp...  6.14 us
    pallas_call x2, Pallas kernels, masked_half(): pl.pallas_call(mask_kernel, in_specs=[smem, smem, vmem], out_specs=vmem,...  3.65 us
  transfers between devices with their start and end apart: 1, of which 1 were waited for; matrix products, arithmetic and copies ran while one was open for 1% of the time, Pallas kernels for 1%

profile of v8, /device:TPU:1, one launch (start us, length us, event | category | flops | bytes accessed | tf_op | source)
XLA Modules:
  0.0 141.5 jit_solution(14084026156070725830)
XLA Ops:
  7.2 0.0 all-gather.5.cloned.1.call-start
  7.2 1.8 %shard_map.59 = bf16[512,256]{1,0:T(8,128)(2,1)} custom-call(s32[1]{0:T(128)} %bitcast.layer_ref, s32[4,4]{1,0:T(4,128)} %mask_ref.2, bf16[512,512]{1,0:T(8,128)(2,1)} %matrix_ref.2), custom_call_target="tpu_custom_call" | custom-call | bytes 786432 | tf_op jit(solution)/shard_map/pallas_call | solution.py:32
  9.0 0.0 all-gather.5.cloned.1.call-update
  9.1 1.8 %shard_map.60 = bf16[512,256]{1,0:T(8,128)(2,1)} custom-call(s32[1]{0:T(128)} %bitcast.layer_ref, s32[4,4]{1,0:T(4,128)} %mask_ref.3, bf16[512,512]{1,0:T(8,128)(2,1)} %matrix_ref.3), custom_call_target="tpu_custom_call" | custom-call | bytes 786432 | tf_op jit(solution)/shard_map/pallas_call | solution.py:32
  10.9 1.3 broadcast_in_dim.8
  12.2 56.0 %all_to_all.10 = bf16[16,512,256]{2,1,0:T(8,128)(2,1)} all-to-all(bf16[16,512,256]{2,1,0:T(8,128)(2,1)S(1)} %broadcast_in_dim.8), channel_id=1, replica_groups=mesh['row'=16,'col'=16,'depth'=2] {'row'}, dimensions={0} | all-to-all | bytes 8388608 | tf_op jit(solution)/shard_map/all_to_all | solution.py:131
  68.2 27.4 %all-gather.5.cloned.1.call-done = bf16[16384,256]{1,0:T(8,128)(2,1)} async-done(((bf16[512,256]{1,0:T(8,128)(2,1)}), bf16[16384,256]{1,0:T(8,128)(2,1)}) %all-gather.5.cloned.1.call-update) | async-done | bytes 8388624 | tf_op jit(solution)/shard_map/all_gather | solution.py:128
  95.6 6.1 %shard_map.61 = (bf16[512,256]{1,0:T(8,128)(2,1)}, f32[64,1,128]{2,1,0:T(1,128)}) custom-call(bf16[32,512,256]{2,1,0:T(8,128)(2,1)} %bitcast.5, bf16[32,256,256]{2,1,0:T(8,128)(2,1)} %bitcast.4), custom_call_target="tpu_custom_call" | custom-call | flops 2147483648 | bytes 12582912 | tf_op jit(solution)/shard_map/pallas_call | solution.py:81
  101.8 16.5 %all_to_all.11 = f32[64,1,128]{2,1,0:T(1,128)S(1)} all-to-all(f32[64,1,128]{2,1,0:T(1,128)} %get-tuple-element.5), channel_id=1, replica_groups={{0,1,2,3,32,33,34,35,64,65,66,67,96,97,98,99,128,129,130,131,160,161,16..., dimensions={0} | all-to-all | bytes 65536 | tf_op jit(solution)/shard_map/all_to_all | solution.py:114
  118.2 0.1 reduce_sum.18
  118.3 13.9 %all-gather.2 = f32[8,1,128]{2,1,0:T(1,128)S(1)} all-gather(f32[1,1,128]{2,1,0:T(1,128)S(1)} %bitcast.6), channel_id=3, replica_groups={{0,4,8,12,16,20,24,28},{2,6,10,14,18,22,26,30},{1,5,9,13,17,21,25,29},{..., dimensions={0}, use_global_device_ids=true | all-gather | bytes 4608 | tf_op jit(solution)/shard_map/all_gather | solution.py:119
  132.2 0.6 reduce.1
Async XLA Ops:
  7.2 88.5 %all-gather.5.cloned.1.call-start = ((), (), s32[]{:S(2)}) async-start(), calls=%async_computation.2 | async-start | bytes 8650752 | tf_op jit(solution)/shard_map/all_gather | solution.py:128
Sparse Core Ops, SparseCore 0:
  10.7 84.8 all-gather.4
